TPU v7x, 512 devices: a whole 4x8x8 slice. The times are simulated.
512 devices in a mesh: col: 8 (over x, core), row: 64 (over y, z).
Axes of the slice: x: 4, y: 8, z: 8, core: 2. Of those that a mesh axis runs over, the one named last changes fastest.
Arguments:
- frames: bfloat16 [1536, 65536], P(('col', 'row')), as said below
- frame_order: int32 [1536], P('col'), may hold values from 0 to 191, as said below
Outputs:
- rotated: bfloat16 [1536, 65536], P('col', 'row')
Inputs may be any that keep to these rules, and one draw needn't show every extreme that they name: `frame_order`: each aligned run of 192 entries is a permutation of 0 to 191. `frames`: frames have scales that differ from frame to frame and pixel to pixel.
All inputs are finite; a program needn't handle non-finite values.
Results may differ from a plain program's by a relative error of at most 0.015.
The roundings to bfloat16 on the way count: a program that leaves them out, or rounds other values in their place, can miss the bound.
Values may be sent and summed in bfloat16 or wider, within the bound.
No kernel may reach another device: no remote copies, remote signals or barrier semaphores. Data moves between devices by JAX's collectives and lax.ppermute only.
A program may use at most 64 MiB of HBM per device.

v0:
```python
import jax
import jax.numpy as jnp
from jax import lax
from jax.sharding import PartitionSpec as P

BLOCK = 48
ROUNDS = 4


def passed_along(value, axis, steps):
    count = lax.axis_size(axis)
    pairs = [(source, (source + steps) % count) for source in range(count)]
    return lax.ppermute(value, axis, pairs)


def rotation(gram):
    diag = jnp.diagonal(gram)
    gap = diag[None, :] - diag[:, None]
    total = diag[None, :] + diag[:, None]
    theta = gram * gap / (gap * gap + 4.0 * gram * gram + 0.01 * total * total)
    term = theta / 64.0
    result = jnp.eye(theta.shape[0], dtype=jnp.float32) + term
    power = term
    for order in range(2, 7):
        power = jnp.dot(power, term, precision=lax.Precision.HIGHEST) / float(order)
        result = result + power
    for square in range(6):
        result = jnp.dot(result, result, precision=lax.Precision.HIGHEST)
    return result


def on_device(frames, frame_order):
    row_count = lax.axis_size("row")
    slots = frame_order.shape[0]
    width = frames.shape[1] // row_count
    arrived = lax.all_to_all(frames, "row", split_axis=1, concat_axis=0, tiled=True)
    data = jnp.take(arrived, frame_order, axis=0)
    pair_rows = 2 * BLOCK
    for step in range(ROUNDS):
        pairs = data.reshape(2, pair_rows, width)
        partial_grams = jnp.einsum("pir,pjr->pij", pairs, pairs, preferred_element_type=jnp.float32)
        grams = lax.psum(partial_grams, "row")
        rotors = jax.vmap(rotation)(grams).astype(jnp.bfloat16)
        turned = jnp.einsum(
            "pki,pkr->pir", rotors, pairs, preferred_element_type=jnp.float32
        ).astype(jnp.bfloat16)
        blocks = turned.reshape(4, BLOCK, width)
        if step + 1 < ROUNDS:
            from_left = passed_along(blocks[2], "col", 1)
            from_right = passed_along(blocks[1], "col", -1)
            blocks = jnp.stack([from_left, blocks[3], blocks[0], from_right])
        data = blocks.reshape(slots, width)
    return data


def solution(mesh):
    placed = (P(("col", "row"), None), P("col"))
    return jax.shard_map(
        on_device, mesh=mesh, in_specs=placed, out_specs=P("col", "row"), check_vma=False
    )
```

profile of v0, /device:TPU:1, one launch (start us, length us, event | category | flops | bytes accessed | tf_op | source)
XLA Modules:
  0.0 693.3 jit_solution(526172951026781345)
XLA Ops:
  6.5 17.1 %all-to-all-start = ((bf16[3,64,1024]{2,0,1:T(4,128)(2,1)}), bf16[3,64,1024]{2,0,1:T(4,128)(2,1)S(1)}, u32[]{:S(2)}, u32[]{:S(2)}) async-start(bf16[3,64,1024]{2,0,1:T(4,128)(2,1)} %bitcast.123), calls=%async_computation | async-start | bytes 1048576 | tf_op jit(solution)/shard_map/all_to_all | solution.py:36
  23.7 0.7 compare_and_fusion
  24.5 0.7 compare_select_fusion
  25.2 14.8 %all-to-all-done = bf16[3,64,1024]{2,0,1:T(4,128)(2,1)S(1)} async-done(((bf16[3,64,1024]{2,0,1:T(4,128)(2,1)}), bf16[3,64,1024]{2,0,1:T(4,128)(2,1)S(1)}, u32[]{:S(2)}, u32[]{:S(2)}) %all-to-all-start) | async-done | bytes 393248 | tf_op jit(solution)/shard_map/all_to_all | solution.py:36
  40.4 1.0 gather_fusion
  41.4 1.0 fusion.4
  42.5 143.0 %all-reduce.5.cloned.1.call-done = f32[2,96,96]{2,1,0:T(8,128)} async-done(((f32[2,96,96]{2,1,0:T(8,128)}), f32[2,96,96]{2,1,0:T(8,128)}) %all-reduce.5.cloned.1.call-update) | async-done | bytes 73744 | tf_op jit(solution)/shard_map/psum | solution.py:42
  185.5 3.7 copy.17
  189.2 2.9 gather_fusion.1
  192.2 0.4 convolution_multiply_fusion.19
  195.9 5.4 collective-permute-start
  201.3 1.6 collective-permute-done
  203.0 2.4 collective-permute-done.1
  205.4 0.9 fusion.51
  206.4 142.6 %all-reduce.7.cloned.1.call-done = f32[2,96,96]{2,1,0:T(8,128)} async-done(((f32[2,96,96]{2,1,0:T(8,128)}), f32[2,96,96]{2,1,0:T(8,128)}) %all-reduce.7.cloned.1.call-update) | async-done | bytes 73744 | tf_op jit(solution)/shard_map/psum | solution.py:42
  349.0 3.7 copy.20
  352.7 2.9 gather_fusion.2
  359.3 5.4 collective-permute-start.2
  364.8 1.6 collective-permute-done.2
  366.4 2.4 collective-permute-done.3
  368.8 0.9 fusion.57
  370.0 142.4 %all-reduce.9.cloned.1.call-done = f32[2,96,96]{2,1,0:T(8,128)} async-done(((f32[2,96,96]{2,1,0:T(8,128)}), f32[2,96,96]{2,1,0:T(8,128)}) %all-reduce.9.cloned.1.call-update) | async-done | bytes 73744 | tf_op jit(solution)/shard_map/psum | solution.py:42
  512.4 3.7 copy.23
  516.1 2.9 gather_fusion.3
  522.7 5.5 collective-permute-start.4
  528.2 1.6 collective-permute-done.4
  529.8 2.4 collective-permute-done.5
  532.3 0.9 fusion.63
  533.2 142.6 %all-reduce.11.cloned.1.call-done = f32[2,96,96]{2,1,0:T(8,128)} async-done(((f32[2,96,96]{2,1,0:T(8,128)}), f32[2,96,96]{2,1,0:T(8,128)}) %all-reduce.11.cloned.1.call-update) | async-done | bytes 73744 | tf_op jit(solution)/shard_map/psum | solution.py:42
  675.8 3.7 copy.26
  679.5 2.9 gather_fusion.4
  685.8 1.0 convolution_convert_fusion
  (80 shorter events, 14.8 us)
Async XLA Ops:
  6.5 33.5 %all-to-all-start = ((bf16[3,64,1024]{2,0,1:T(4,128)(2,1)}), bf16[3,64,1024]{2,0,1:T(4,128)(2,1)S(1)}, u32[]{:S(2)}, u32[]{:S(2)}) async-start(bf16[3,64,1024]{2,0,1:T(4,128)(2,1)} %bitcast.123), calls=%async_computation | async-start | bytes 1048576 | tf_op jit(solution)/shard_map/all_to_all | solution.py:36
  23.7 161.8 %all-reduce.5.cloned.1.call-start = ((), (), s32[]{:S(2)}) async-start(), calls=%async_computation.1 | async-start | bytes 196608 | tf_op jit(solution)/shard_map/psum | solution.py:42
  42.4 306.6 %all-reduce.7.cloned.1.call-start = ((), (), s32[]{:S(2)}) async-start(), calls=%async_computation.2 | async-start | bytes 196608 | tf_op jit(solution)/shard_map/psum | solution.py:42
  185.5 6.7 copy-start
  195.9 7.1 %collective-permute-start = (bf16[48,1024]{1,0:T(8,128)(2,1)S(1)}, bf16[48,1024]{1,0:T(8,128)(2,1)S(1)}, u32[]{:S(2)}, u32[]{:S(2)}) collective-permute-start(bf16[48,1024]{1,0:T(8,128)(2,1)S(1)} %get-tuple-element.13), channel_id=1, source_target_pairs={{0,64},{64,128},{128,192},{192,256},{256,320},{320,384},{384,448},... | collective-permute-start | bytes 294920 | tf_op jit(solution)/shard_map/ppermute | solution.py:13
  201.3 4.0 collective-permute-start.1
  206.4 306.0 %all-reduce.9.cloned.1.call-start = ((), (), s32[]{:S(2)}) async-start(), calls=%async_computation.3 | async-start | bytes 196608 | tf_op jit(solution)/shard_map/psum | solution.py:42
  349.0 6.7 copy-start.1
  359.3 7.1 %collective-permute-start.2 = (bf16[48,1024]{1,0:T(8,128)(2,1)S(1)}, bf16[48,1024]{1,0:T(8,128)(2,1)S(1)}, u32[]{:S(2)}, u32[]{:S(2)}) collective-permute-start(bf16[48,1024]{1,0:T(8,128)(2,1)S(1)} %get-tuple-element.9), channel_id=1, source_target_pairs={{0,64},{64,128},{128,192},{192,256},{256,320},{320,384},{384,448},... | collective-permute-start | bytes 294920 | tf_op jit(solution)/shard_map/ppermute | solution.py:13
  364.8 4.0 collective-permute-start.3
  369.8 306.0 %all-reduce.11.cloned.1.call-start = ((), (), s32[]{:S(2)}) async-start(), calls=%async_computation.4 | async-start | bytes 196608 | tf_op jit(solution)/shard_map/psum | solution.py:42
  512.4 6.7 copy-start.2
  522.7 7.1 %collective-permute-start.4 = (bf16[48,1024]{1,0:T(8,128)(2,1)S(1)}, bf16[48,1024]{1,0:T(8,128)(2,1)S(1)}, u32[]{:S(2)}, u32[]{:S(2)}) collective-permute-start(bf16[48,1024]{1,0:T(8,128)(2,1)S(1)} %get-tuple-element.5), channel_id=1, source_target_pairs={{0,64},{64,128},{128,192},{192,256},{256,320},{320,384},{384,448},... | collective-permute-start | bytes 294920 | tf_op jit(solution)/shard_map/ppermute | solution.py:13
  528.2 4.0 collective-permute-start.5
  675.8 6.7 copy-start.3
Sparse Core Ops, SparseCore 0:
  42.5 142.9 all-reduce.4
  206.5 142.4 all-reduce.6
  369.9 142.4 all-reduce.8
  533.3 142.3 all-reduce.10
where the time goes:
time: 697 us; the launch traced here: 693 us
  waiting for transfers between devices  598 us (86%)
  starting transfers between devices  33.8 us (5%)
  local copies, waits for them, and re-layouts  28.3 us (4%)
  matrix products  18.5 us (3%)
  between operations  13.6 us (2%)
    psum x4, waiting for transfers between devices, on_device(): grams = lax.psum(partial_grams, 'row')  571 us
    all_to_all x1, starting transfers between devices, on_device(): lax.all_to_all(frames, 'row', split_axis=1, concat_axis=0, tiled=True)  17.1 us
    ppermute x6, starting transfers between devices, passed_along(): return lax.ppermute(value, axis, pairs)  16.4 us
    psum x4, local copies, waits for them, and re-layouts, on_device(): grams = lax.psum(partial_grams, 'row')  14.9 us
    all_to_all x1, waiting for transfers between devices, on_device(): lax.all_to_all(frames, 'row', split_axis=1, concat_axis=0, tiled=True)  14.8 us
  transfers between devices with their start and end apart: 11, of which 11 were waited for; matrix products, arithmetic and copies ran while one was open for 0% of the time, Pallas kernels for 0%

commit v1 on v0

v1 whole, which is shorter than its diff:
```python
import functools

import jax
import jax.numpy as jnp
from jax import lax
from jax.experimental import pallas as pl
from jax.experimental.pallas import tpu as pltpu
from jax.sharding import PartitionSpec as P

BLOCK = 48
PAIR = 2 * BLOCK
LANES = 128
SPAN = 4
SLOTS = 15
CHUNK = LANES - PAIR

CARRIERS = [(c, s, t) for c in range(2) for s in range(SPAN) for t in range(s + 1, SPAN)]
CARRIERS += [(0, 0, 0), (0, 1, 1), (0, 2, 2)]
SPREAD = [(0, 3, 3), (1, 0, 0), (1, 1, 1), (1, 2, 2), (1, 3, 3)]


def passed_along(value, axis, steps):
    count = lax.axis_size(axis)
    pairs = [(source, (source + steps) % count) for source in range(count)]
    return lax.ppermute(value, axis, pairs)


def iota(shape, dim):
    return lax.broadcasted_iota(jnp.int32, shape, dim)


def mm(a, b):
    return jnp.dot(a, b, preferred_element_type=jnp.float32)


def mm_nt(a, b):
    return lax.dot_general(a, b, (((1,), (1,)), ((), ())), preferred_element_type=jnp.float32)


def halves(value):
    high = value.astype(jnp.bfloat16)
    low = (value - high.astype(jnp.float32)).astype(jnp.bfloat16)
    return high, low


def fill(rows_ref, own, prev, after, prev2, after2):
    width = own.shape[1]
    pieces = [
        [prev[0:PAIR], own[0:PAIR], after[0:PAIR], after2[...]],
        [prev2[...], prev[PAIR:], own[PAIR:], after[PAIR:]],
    ]
    for c in range(2):
        for s in range(SPAN):
            rows_ref[c, s, 0:PAIR, :] = pieces[c][s]
            rows_ref[c, s, PAIR:, :] = jnp.zeros((CHUNK, width), jnp.bfloat16)


def gram_kernel(own, prev, after, prev2, after2, packed, rows_ref):
    width = own.shape[1]
    fill(rows_ref, own, prev, after, prev2, after2)
    block = {}
    for c in range(2):
        for s in range(SPAN):
            right = rows_ref[c, s:SPAN].reshape((SPAN - s) * LANES, width)
            strip = mm_nt(rows_ref[c, s, 0:PAIR, :], right)
            for t in range(s, SPAN):
                block[c, s, t] = strip[:, (t - s) * LANES : (t - s + 1) * LANES]
    lane = iota((PAIR, LANES), 1)
    for k in range(SLOTS):
        extra = pltpu.roll(block[SPREAD[k // 3]], PAIR - CHUNK * (k % 3), 1)
        packed[k * PAIR : (k + 1) * PAIR, :] = jnp.where(lane < PAIR, block[CARRIERS[k]], extra)
    tail = packed.shape[0] - SLOTS * PAIR
    if tail:
        packed[SLOTS * PAIR :, :] = jnp.zeros((tail, LANES), jnp.float32)


def product(a, b):
    ah, al = a
    bh, bl = b
    wide = mm(jnp.concatenate([ah, al], axis=0), jnp.concatenate([bh, bl], axis=1))
    return wide[:LANES, :LANES] + (wide[LANES:, :LANES] + wide[:LANES, LANES:])


def turned_rotors(grams):
    shape = (LANES, LANES)
    row, lane = iota(shape, 0), iota(shape, 1)
    inside = (row < PAIR) & (lane < PAIR)
    eye = ((row == lane) & inside).astype(jnp.float32)
    terms = []
    for gram in grams:
        picked = gram * eye
        down = jnp.sum(picked, axis=1, keepdims=True)
        along = jnp.sum(picked, axis=0, keepdims=True)
        gap = along - down
        total = along + down
        bottom = gap * gap + 4.0 * gram * gram + 0.01 * total * total
        theta = gram * gap / jnp.where(inside, bottom, 1.0)
        terms.append(jnp.where(inside, theta, 0.0) * (-1.0 / 64.0))
    first = [halves(e) for e in terms]
    second = [product(a, a) for a in first]
    third = [product(halves(e2), a) for e2, a in zip(second, first)]
    result = []
    for e, e2, e3 in zip(terms, second, third):
        rest = e * (1.0 / 24.0) + e2 * (1.0 / 120.0) + e3 * (1.0 / 720.0)
        result.append(e + e2 * 0.5 + e3 * (1.0 / 6.0) + product(halves(e3), halves(rest)))
    for _ in range(6):
        split = [halves(d) for d in result]
        result = [2.0 * d + product(a, a) for d, a in zip(result, split)]
    return [(d + eye).astype(jnp.bfloat16) for d in result]


def rounds_kernel(packed, own, prev, after, prev2, after2, out, rows_ref):
    width = own.shape[1]
    fill(rows_ref, own, prev, after, prev2, after2)
    lane = iota((PAIR, LANES), 1)
    floor = jnp.zeros((CHUNK, LANES), jnp.float32)
    gram = {}
    slot = [packed[k * PAIR : (k + 1) * PAIR, :] for k in range(SLOTS)]
    for k, name in enumerate(CARRIERS):
        gram[name] = jnp.concatenate([jnp.where(lane < PAIR, slot[k], 0.0), floor], axis=0)
    for m, name in enumerate(SPREAD):
        value = jnp.zeros((PAIR, LANES), jnp.float32)
        for j in range(3):
            moved = pltpu.roll(slot[3 * m + j], (CHUNK * j - PAIR) % LANES, 1)
            value = jnp.where((lane >= CHUNK * j) & (lane < CHUNK * (j + 1)), moved, value)
        gram[name] = jnp.concatenate([value, floor], axis=0)
    top_lane = iota((LANES, LANES), 1) < BLOCK
    top_half = iota((BLOCK, LANES), 1) < BLOCK
    count = SPAN
    while True:
        names = [(c, s) for c in range(2) for s in range(count)]
        turned = dict(zip(names, turned_rotors([gram[c, s, s] for c, s in names])))
        if count == 1:
            break
        following = {}
        for c in range(2):
            right = {}
            for t in range(count):
                stack = []
                for s in range(t + 1):
                    stack += halves(gram[c, s, t])
                both = mm_nt(jnp.concatenate(stack, axis=0), turned[c, t])
                for s in range(t + 1):
                    at = 2 * s * LANES
                    right[s, t] = both[at : at + LANES] + both[at + LANES : at + 2 * LANES]

            def left(rows, value):
                high, low = halves(value)
                both = mm(rows, jnp.concatenate([high, low], axis=1))
                return both[:, :LANES] + both[:, LANES:]

            for i in range(count - 1):
                upper = turned[c, i][0:BLOCK]
                lower = turned[c, i + 1][BLOCK:PAIR]
                for j in range(i, count - 1):
                    top = left(upper, jnp.where(top_lane, right[i, j], right[i, j + 1]))
                    if i == j:
                        bottom = left(lower, right[i + 1, j + 1])
                        padded = jnp.concatenate(
                            [top, jnp.zeros((LANES - BLOCK, LANES), jnp.float32)], axis=0
                        )
                        bottom = jnp.where(top_half, padded.T[BLOCK:PAIR], bottom)
                    else:
                        bottom = left(lower, jnp.where(top_lane, right[i + 1, j], right[i + 1, j + 1]))
                    following[c, i, j] = jnp.concatenate([top, bottom, floor], axis=0)
            for i in range(count):
                old = rows_ref[c, i]
                if i > 0:
                    lower = turned[c, i][BLOCK:PAIR]
                    rows_ref[c, i - 1, BLOCK:PAIR, :] = mm(lower, old).astype(jnp.bfloat16)
                if i < count - 1:
                    upper = turned[c, i][0:BLOCK]
                    rows_ref[c, i, 0:BLOCK, :] = mm(upper, old).astype(jnp.bfloat16)
        gram = following
        count -= 1
    for c in range(2):
        last = mm(turned[c, 0][0:PAIR], rows_ref[c, 0]).astype(jnp.bfloat16)
        out[(1 - c) * PAIR : (2 - c) * PAIR, :] = last


def on_device(frames, frame_order):
    row_count = lax.axis_size("row")
    width = frames.shape[1] // row_count
    arrived = lax.all_to_all(frames, "row", split_axis=1, concat_axis=0, tiled=True)
    own = jnp.take(arrived, frame_order, axis=0)
    prev = passed_along(own, "col", 1)
    after = passed_along(own, "col", -1)
    prev2 = passed_along(own[PAIR:], "col", 2)
    after2 = passed_along(own[:PAIR], "col", -2)
    held = (own, prev, after, prev2, after2)
    share = -(-SLOTS * PAIR // (8 * row_count)) * 8
    limit = pltpu.CompilerParams(vmem_limit_bytes=48 * 1024 * 1024)
    scratch = [pltpu.VMEM((2, SPAN, LANES, width), jnp.bfloat16)]
    packed = pl.pallas_call(
        gram_kernel,
        out_shape=jax.ShapeDtypeStruct((share * row_count, LANES), jnp.float32),
        scratch_shapes=scratch,
        compiler_params=limit,
        name="grams",
    )(*held)
    parts = packed.reshape(row_count, share, LANES)
    parts = lax.all_to_all(parts, "row", split_axis=0, concat_axis=0, tiled=True)
    summed = jnp.sum(parts, axis=0)
    copies = jnp.broadcast_to(summed[None], (row_count, share, LANES))
    whole = lax.all_to_all(copies, "row", split_axis=0, concat_axis=0, tiled=True)
    return pl.pallas_call(
        rounds_kernel,
        out_shape=jax.ShapeDtypeStruct((4 * BLOCK, width), jnp.bfloat16),
        scratch_shapes=scratch,
        compiler_params=limit,
        name="rounds",
    )(whole.reshape(row_count * share, LANES), *held)


def solution(mesh):
    placed = (P(("col", "row"), None), P("col"))
    return jax.shard_map(
        on_device, mesh=mesh, in_specs=placed, out_specs=P("col", "row"), check_vma=False
    )
```

time: 697 us -> 128 us (0.18)
  the two profiles are of different devices: /device:TPU:1 before, /device:TPU:16 now
where the time goes in v1:
time: 128 us
  blocking collectives  60.8 us (48%)
  waiting for transfers between devices  27.3 us (21%)
  starting transfers between devices  23.7 us (19%)
  Pallas kernels  14.6 us (11%)
  local copies, waits for them, and re-layouts  1.43 us (1%)
    all_to_all x1, blocking collectives, on_device(): lax.all_to_all(parts, 'row', split_axis=0, concat_axis=0, tiled=True)  30.9 us
    all_to_all x1, blocking collectives, on_device(): lax.all_to_all(copies, 'row', split_axis=0, concat_axis=0, tiled=True)  29.9 us
    all_to_all x1, waiting for transfers between devices, on_device(): lax.all_to_all(frames, 'row', split_axis=1, concat_axis=0, tiled=True)  19.4 us
    all_to_all x1, starting transfers between devices, on_device(): lax.all_to_all(frames, 'row', split_axis=1, concat_axis=0, tiled=True)  16.6 us
    pallas_call x1, Pallas kernels, on_device(): pl.pallas_call(rounds_kernel, out_shape=jax.ShapeDtypeStruct((4 * BLOCK,...  12.8 us
    ppermute x4, waiting for transfers between devices, passed_along(): return lax.ppermute(value, axis, pairs)  7.96 us
    ppermute x4, starting transfers between devices, passed_along(): return lax.ppermute(value, axis, pairs)  7.11 us
  transfers between devices with their start and end apart: 5, of which 3 were waited for; matrix products, arithmetic and copies ran while one was open for 0% of the time, Pallas kernels for 0%

profile of v1, /device:TPU:16, one launch (start us, length us, event | category | flops | bytes accessed | tf_op | source)
XLA Modules:
  0.0 128.2 jit_solution(12481389808983952283)
XLA Ops:
  0.0 0.0 copy-start
  0.0 16.6 %all-to-all-start = ((bf16[3,64,1024]{2,0,1:T(4,128)(2,1)}), bf16[3,64,1024]{2,0,1:T(4,128)(2,1)S(1)}, u32[]{:S(2)}, u32[]{:S(2)}) async-start(bf16[3,64,1024]{2,0,1:T(4,128)(2,1)} %bitcast.7), calls=%async_computation | async-start | bytes 1048576 | tf_op jit(solution)/shard_map/all_to_all | solution.py:184
  16.6 0.0 copy-done
  16.7 19.4 %all-to-all-done = bf16[3,64,1024]{2,0,1:T(4,128)(2,1)S(1)} async-done(((bf16[3,64,1024]{2,0,1:T(4,128)(2,1)}), bf16[3,64,1024]{2,0,1:T(4,128)(2,1)S(1)}, u32[]{:S(2)}, u32[]{:S(2)}) %all-to-all-start) | async-done | bytes 393248 | tf_op jit(solution)/shard_map/all_to_all | solution.py:184
  36.0 0.3 all_to_all.23
  36.4 1.0 gather_fusion
  37.4 0.1 broadcast_select_fusion.own
  37.5 0.2 collective-permute-start.1
  37.7 0.3 collective-permute-start
  38.0 4.7 %collective-permute-start.3 = (bf16[96,1024]{1,0:T(8,128)(2,1)S(1)}, bf16[96,1024]{1,0:T(8,128)(2,1)S(1)}, u32[]{:S(2)}, u32[]{:S(2)}) collective-permute-start(bf16[96,1024]{1,0:T(8,128)(2,1)S(1)} %get-tuple-element.5), channel_id=1, source_target_pairs={{0,384},{64,448},{128,0},{192,64},{256,128},{320,192},{384,256},{4... | collective-permute-start | bytes 589832 | tf_op jit(solution)/shard_map/ppermute | solution.py:25
  42.7 1.9 %collective-permute-start.2 = (bf16[96,1024]{1,0:T(8,128)(2,1)S(1)}, bf16[96,1024]{1,0:T(8,128)(2,1)S(1)}, u32[]{:S(2)}, u32[]{:S(2)}) collective-permute-start(bf16[96,1024]{1,0:T(8,128)(2,1)S(1)} %get-tuple-element.6), channel_id=1, source_target_pairs={{0,128},{64,192},{128,256},{192,320},{256,384},{320,448},{384,0},{... | collective-permute-start | bytes 589832 | tf_op jit(solution)/shard_map/ppermute | solution.py:25
  44.6 4.3 %collective-permute-done.3.after2 = bf16[96,1024]{1,0:T(8,128)(2,1)S(1)} collective-permute-done((bf16[96,1024]{1,0:T(8,128)(2,1)S(1)}, bf16[96,1024]{1,0:T(8,128)(2,1)S(1)}, u32[]{:S(2)}, u32[]{:S(2)}) %collective-permute-start.3) | collective-permute-done | bytes 196640 | tf_op jit(solution)/shard_map/ppermute | solution.py:25
  49.0 3.6 %collective-permute-done.2.prev2 = bf16[96,1024]{1,0:T(8,128)(2,1)S(1)} collective-permute-done((bf16[96,1024]{1,0:T(8,128)(2,1)S(1)}, bf16[96,1024]{1,0:T(8,128)(2,1)S(1)}, u32[]{:S(2)}, u32[]{:S(2)}) %collective-permute-start.2) | collective-permute-done | bytes 196640 | tf_op jit(solution)/shard_map/ppermute | solution.py:25
  52.6 0.0 collective-permute-done.1.after
  52.6 0.0 collective-permute-done.prev
  52.6 1.8 %grams.1 = f32[1536,128]{1,0:T(8,128)S(1)} custom-call(bf16[192,1024]{1,0:T(8,128)(2,1)S(1)} %broadcast_select_fusion.own, bf16[192,1024]{1,0:T(8,128)(2,1)S(1)} %collective-permute-done.prev, bf16[192,1024]{1,0:T(8,128)(2,1)S(1)} %collective-permute-done.1.after, bf16[96,1024]{1,0:T(8,128)(2,1)S(1)} %collective-permute-done.2.prev2, ...), custom_call_target="tpu_custom_call" | custom-call | tf_op jit(solution)/shard_map/grams/pallas_call | solution.py:194
  54.4 30.9 %all_to_all.29 = f32[64,24,128]{2,1,0:T(8,128)S(1)} all-to-all(f32[64,24,128]{2,1,0:T(8,128)S(1)} %bitcast.5), channel_id=1, replica_groups=mesh['col'=8,'row'=64] {'row'}, dimensions={0} | all-to-all | bytes 1572864 | tf_op jit(solution)/shard_map/all_to_all | solution.py:202
  85.3 0.1 reduce_sum.9
  85.4 0.1 broadcast_in_dim.21
  85.4 29.9 %all_to_all.30 = f32[64,24,128]{2,1,0:T(8,128)S(1)} all-to-all(f32[64,24,128]{2,1,0:T(8,128)S(1)} %broadcast_in_dim.21), channel_id=1, replica_groups=mesh['col'=8,'row'=64] {'row'}, dimensions={0} | all-to-all | bytes 1572864 | tf_op jit(solution)/shard_map/all_to_all | solution.py:205
  115.4 12.8 %rounds.1 = bf16[192,1024]{1,0:T(8,128)(2,1)} custom-call(f32[1536,128]{1,0:T(8,128)S(1)} %bitcast.4, bf16[192,1024]{1,0:T(8,128)(2,1)S(1)} %broadcast_select_fusion.own, bf16[192,1024]{1,0:T(8,128)(2,1)S(1)} %collective-permute-done.prev, bf16[192,1024]{1,0:T(8,128)(2,1)S(1)} %collective-permute-done.1.after, ...), custom_call_target="tpu_custom_call" | custom-call | tf_op jit(solution)/shard_map/rounds/pallas_call | solution.py:206
  (4 shorter events, 0.0 us)
Async XLA Ops:
  0.0 16.6 %copy-start = (s32[192]{0:T(256)S(1)}, s32[192]{0:T(256)}, u32[]{:S(2)}) copy-start(s32[192]{0:T(256)} %param.3) | copy-start | bytes 2308
  0.0 36.0 %all-to-all-start = ((bf16[3,64,1024]{2,0,1:T(4,128)(2,1)}), bf16[3,64,1024]{2,0,1:T(4,128)(2,1)S(1)}, u32[]{:S(2)}, u32[]{:S(2)}) async-start(bf16[3,64,1024]{2,0,1:T(4,128)(2,1)} %bitcast.7), calls=%async_computation | async-start | bytes 1048576 | tf_op jit(solution)/shard_map/all_to_all | solution.py:184
  37.5 15.1 %collective-permute-start.1 = (bf16[192,1024]{1,0:T(8,128)(2,1)S(1)}, bf16[192,1024]{1,0:T(8,128)(2,1)S(1)}, u32[]{:S(2)}, u32[]{:S(2)}) collective-permute-start(bf16[192,1024]{1,0:T(8,128)(2,1)S(1)} %broadcast_select_fusion.own), channel_id=1, source_target_pairs={{0,448},{64,0},{128,64},{192,128},{256,192},{320,256},{384,320},{4... | collective-permute-start | bytes 1179656 | tf_op jit(solution)/shard_map/ppermute | solution.py:25
  37.7 14.9 %collective-permute-start = (bf16[192,1024]{1,0:T(8,128)(2,1)S(1)}, bf16[192,1024]{1,0:T(8,128)(2,1)S(1)}, u32[]{:S(2)}, u32[]{:S(2)}) collective-permute-start(bf16[192,1024]{1,0:T(8,128)(2,1)S(1)} %broadcast_select_fusion.own), channel_id=1, source_target_pairs={{0,64},{64,128},{128,192},{192,256},{256,320},{320,384},{384,448},... | collective-permute-start | bytes 1179656 | tf_op jit(solution)/shard_map/ppermute | solution.py:25
  38.0 10.9 %collective-permute-start.3 = (bf16[96,1024]{1,0:T(8,128)(2,1)S(1)}, bf16[96,1024]{1,0:T(8,128)(2,1)S(1)}, u32[]{:S(2)}, u32[]{:S(2)}) collective-permute-start(bf16[96,1024]{1,0:T(8,128)(2,1)S(1)} %get-tuple-element.5), channel_id=1, source_target_pairs={{0,384},{64,448},{128,0},{192,64},{256,128},{320,192},{384,256},{4... | collective-permute-start | bytes 589832 | tf_op jit(solution)/shard_map/ppermute | solution.py:25
  42.7 9.9 %collective-permute-start.2 = (bf16[96,1024]{1,0:T(8,128)(2,1)S(1)}, bf16[96,1024]{1,0:T(8,128)(2,1)S(1)}, u32[]{:S(2)}, u32[]{:S(2)}) collective-permute-start(bf16[96,1024]{1,0:T(8,128)(2,1)S(1)} %get-tuple-element.6), channel_id=1, source_target_pairs={{0,128},{64,192},{128,256},{192,320},{256,384},{320,448},{384,0},{... | collective-permute-start | bytes 589832 | tf_op jit(solution)/shard_map/ppermute | solution.py:25

commit v2 on v0

v2 whole, which is shorter than its diff:
```python
import jax
import jax.numpy as jnp
from jax import lax
from jax.experimental import pallas as pl
from jax.experimental.pallas import tpu as pltpu
from jax.sharding import PartitionSpec as P

BLOCK = 48
PAIR = 2 * BLOCK
LANES = 128
ROUNDS = 4
SPAN = 5
CHUNK = LANES - PAIR

BLOCKS = [(s, t) for s in range(SPAN) for t in range(s + 1, min(s + ROUNDS, SPAN))]
BLOCKS += [(s, s) for s in range(SPAN)]
SLOTS = 10
CARRIERS, SPREAD, LAST = BLOCKS[:SLOTS], BLOCKS[SLOTS : SLOTS + 3], BLOCKS[SLOTS + 3]
USED = SLOTS * PAIR + BLOCK


def iota(shape, dim):
    return lax.broadcasted_iota(jnp.int32, shape, dim)


def mm(a, b):
    return jnp.dot(a, b, preferred_element_type=jnp.float32)


def mm_nt(a, b):
    return lax.dot_general(a, b, (((1,), (1,)), ((), ())), preferred_element_type=jnp.float32)


def halves(value):
    high = value.astype(jnp.bfloat16)
    low = (value - high.astype(jnp.float32)).astype(jnp.bfloat16)
    return high, low


def shifted(value, lanes):
    return pltpu.roll(value, lanes % LANES, 1)


def fill(rows_ref, core, mine, partner, across, left, right):
    first = core[0] == 0
    pieces = [
        left[...],
        jnp.where(first, across[...], partner[...]),
        mine[...],
        jnp.where(first, partner[...], across[...]),
        right[...],
    ]
    for s in range(SPAN):
        rows_ref[s, 0:PAIR, :] = pieces[s]
        rows_ref[s, PAIR:, :] = jnp.zeros((CHUNK, mine.shape[1]), jnp.bfloat16)


def gram_kernel(core, mine, partner, across, left, right, packed, rows_ref):
    width = mine.shape[1]
    fill(rows_ref, core, mine, partner, across, left, right)
    block = {}
    for s in range(SPAN):
        end = min(s + ROUNDS, SPAN)
        others = rows_ref[s:end].reshape((end - s) * LANES, width)
        strip = mm_nt(rows_ref[s, 0:PAIR, :], others)
        for t in range(s, end):
            block[s, t] = strip[:, (t - s) * LANES : (t - s + 1) * LANES]
    lane = iota((PAIR, LANES), 1)
    last = block[LAST]
    for k in range(SLOTS):
        extra = shifted(block[SPREAD[k // 3]], PAIR - CHUNK * (k % 3)) if k < 9 else shifted(last, PAIR)
        packed[k * PAIR : (k + 1) * PAIR, :] = jnp.where(lane < PAIR, block[CARRIERS[k]], extra)
    packed[SLOTS * PAIR : USED, :] = jnp.where(
        lane[:BLOCK] < LANES // 2, shifted(last[:BLOCK], -CHUNK), shifted(last[BLOCK:], CHUNK)
    )
    tail = packed.shape[0] - USED
    if tail:
        packed[USED:, :] = jnp.zeros((tail, LANES), jnp.float32)


def unpacked(packed):
    lane = iota((PAIR, LANES), 1)
    floor = jnp.zeros((CHUNK, LANES), jnp.float32)
    slot = [packed[k * PAIR : (k + 1) * PAIR, :] for k in range(SLOTS)]
    gram = {}
    for k, name in enumerate(CARRIERS):
        gram[name] = jnp.where(lane < PAIR, slot[k], 0.0)
    for m, name in enumerate(SPREAD):
        value = jnp.zeros((PAIR, LANES), jnp.float32)
        for j in range(3):
            here = (lane >= CHUNK * j) & (lane < CHUNK * (j + 1))
            value = jnp.where(here, shifted(slot[3 * m + j], CHUNK * j - PAIR), value)
        gram[name] = value
    rest = packed[SLOTS * PAIR : USED, :]
    sides = jnp.concatenate([shifted(rest, CHUNK), shifted(rest, -CHUNK)], axis=0)
    value = jnp.where(lane < CHUNK, shifted(slot[SLOTS - 1], -PAIR), sides)
    gram[LAST] = jnp.where(lane < PAIR, value, 0.0)
    return {name: jnp.concatenate([value, floor], axis=0) for name, value in gram.items()}


def product(a, b):
    ah, al = a
    bh, bl = b
    wide = mm(jnp.concatenate([ah, al], axis=0), jnp.concatenate([bh, bl], axis=1))
    return wide[:LANES, :LANES] + (wide[LANES:, :LANES] + wide[:LANES, LANES:])


def turned_rotors(grams):
    shape = (LANES, LANES)
    row, lane = iota(shape, 0), iota(shape, 1)
    inside = (row < PAIR) & (lane < PAIR)
    eye = ((row == lane) & inside).astype(jnp.float32)
    terms = []
    for gram in grams:
        picked = gram * eye
        down = jnp.sum(picked, axis=1, keepdims=True)
        along = jnp.sum(picked, axis=0, keepdims=True)
        gap = along - down
        total = along + down
        bottom = gap * gap + 4.0 * gram * gram + 0.01 * total * total
        theta = gram * gap / jnp.where(inside, bottom, 1.0)
        terms.append(jnp.where(inside, theta, 0.0) * (-1.0 / 64.0))
    first = [halves(e) for e in terms]
    second = [product(a, a) for a in first]
    third = [product(halves(e2), a) for e2, a in zip(second, first)]
    result = []
    for e, e2, e3 in zip(terms, second, third):
        rest = e * (1.0 / 24.0) + e2 * (1.0 / 120.0) + e3 * (1.0 / 720.0)
        result.append(e + e2 * 0.5 + e3 * (1.0 / 6.0) + product(halves(e3), halves(rest)))
    for _ in range(6):
        split = [halves(d) for d in result]
        result = [2.0 * d + product(a, a) for d, a in zip(result, split)]
    return [(d + eye).astype(jnp.bfloat16) for d in result]


def turned_from_left(rows, value):
    high, low = halves(value)
    both = mm(rows, jnp.concatenate([high, low], axis=1))
    return both[:, :LANES] + both[:, LANES:]


def next_grams(gram, turned, count, reach):
    top_lane = iota((LANES, LANES), 1) < BLOCK
    top_half = iota((BLOCK, LANES), 1) < BLOCK
    floor = jnp.zeros((CHUNK, LANES), jnp.float32)
    right = {}
    for t in range(count):
        low = max(0, t - reach)
        stack = []
        for s in range(low, t + 1):
            stack += halves(gram[s, t])
        both = mm_nt(jnp.concatenate(stack, axis=0), turned[t])
        for s in range(low, t + 1):
            at = 2 * (s - low) * LANES
            right[s, t] = both[at : at + LANES] + both[at + LANES : at + 2 * LANES]
    following = {}
    for i in range(count - 1):
        upper, lower = turned[i][0:BLOCK], turned[i + 1][BLOCK:PAIR]
        for j in range(i, min(i + reach, count - 1)):
            top = turned_from_left(upper, jnp.where(top_lane, right[i, j], right[i, j + 1]))
            if i == j:
                bottom = turned_from_left(lower, right[i + 1, j + 1])
                empty = jnp.zeros((LANES - BLOCK, LANES), jnp.float32)
                mirrored = jnp.concatenate([top, empty], axis=0).T[BLOCK:PAIR]
                bottom = jnp.where(top_half, mirrored, bottom)
            else:
                bottom = turned_from_left(lower, jnp.where(top_lane, right[i + 1, j], right[i + 1, j + 1]))
            following[i, j] = jnp.concatenate([top, bottom, floor], axis=0)
    return following


def rounds_kernel(core, packed, mine, partner, across, left, right, kept, sent, rows_ref):
    fill(rows_ref, core, mine, partner, across, left, right)
    gram = unpacked(packed)
    for step in range(ROUNDS):
        count, reach = SPAN - step, ROUNDS - 1 - step
        turned = turned_rotors([gram[s, s] for s in range(count)])
        if reach == 0:
            break
        gram = next_grams(gram, turned, count, reach)
        for i in range(count):
            old = rows_ref[i]
            if i > 0:
                lower = turned[i][BLOCK:PAIR]
                rows_ref[i - 1, BLOCK:PAIR, :] = mm(lower, old).astype(jnp.bfloat16)
            if i < count - 1:
                upper = turned[i][0:BLOCK]
                rows_ref[i, 0:BLOCK, :] = mm(upper, old).astype(jnp.bfloat16)
    first = core[0] == 0
    ends = [mm(turned[i][0:PAIR], rows_ref[i]).astype(jnp.bfloat16) for i in range(2)]
    kept[...] = jnp.where(first, ends[0], ends[1])
    sent[...] = jnp.where(first, ends[1], ends[0])


def passed(value, where):
    count = lax.axis_size("col")
    return lax.ppermute(value, "col", [(source, where(source) % count) for source in range(count)])


def on_device(frames, frame_order):
    row_count = lax.axis_size("row")
    width = frames.shape[1] // row_count
    core = lax.axis_index("col") % 2
    arrived = lax.all_to_all(frames, "row", split_axis=1, concat_axis=0, tiled=True)
    order = jnp.where(core == 0, jnp.roll(frame_order, PAIR), frame_order)
    mine = jnp.take(arrived, order[:PAIR], axis=0)
    other = jnp.take(arrived, order[PAIR:], axis=0)
    partner = passed(other, lambda c: c ^ 1)
    across = passed(other, lambda c: c - 1 if c % 2 == 0 else c + 1)
    left = passed(mine, lambda c: c + 2)
    right = passed(mine, lambda c: c - 2)
    held = (mine, partner, across, left, right)
    chosen = core.astype(jnp.int32).reshape(1)
    share = -(-USED // (8 * row_count)) * 8
    limit = pltpu.CompilerParams(vmem_limit_bytes=48 * 1024 * 1024)
    scratch = [pltpu.VMEM((SPAN, LANES, width), jnp.bfloat16)]
    scalar = pl.BlockSpec(memory_space=pltpu.SMEM)
    vector = pl.BlockSpec(memory_space=pltpu.VMEM)
    packed = pl.pallas_call(
        gram_kernel,
        out_shape=jax.ShapeDtypeStruct((share * row_count, LANES), jnp.float32),
        in_specs=[scalar] + [vector] * 5,
        scratch_shapes=scratch,
        compiler_params=limit,
        name="grams",
    )(chosen, *held)
    parts = packed.reshape(row_count, share, LANES)
    parts = lax.all_to_all(parts, "row", split_axis=0, concat_axis=0, tiled=True)
    summed = jnp.sum(parts, axis=0)
    copies = jnp.broadcast_to(summed[None], (row_count, share, LANES))
    whole = lax.all_to_all(copies, "row", split_axis=0, concat_axis=0, tiled=True)
    pair = jax.ShapeDtypeStruct((PAIR, width), jnp.bfloat16)
    kept, sent = pl.pallas_call(
        rounds_kernel,
        out_shape=(pair, pair),
        in_specs=[scalar] + [vector] * 6,
        scratch_shapes=scratch,
        compiler_params=limit,
        name="rounds",
    )(chosen, whole.reshape(row_count * share, LANES), *held)
    got = passed(sent, lambda c: c ^ 1)
    upper = jnp.where(core == 0, kept, got)
    lower = jnp.where(core == 0, got, kept)
    return jnp.concatenate([upper, lower], axis=0)


def solution(mesh):
    placed = (P(("col", "row"), None), P("col"))
    return jax.shard_map(
        on_device, mesh=mesh, in_specs=placed, out_specs=P("col", "row"), check_vma=False
    )
```

time: 697 us -> 120 us (0.17)
  waiting for transfers between devices: 598 us -> 23.9 us
  blocking collectives: 0 us -> 43.1 us
  local copies, waits for them, and re-layouts: 28.3 us -> 2.01 us
  matrix products: 18.5 us -> 0 us
  between operations: 13.6 us -> 0.14 us
  Pallas kernels: 0 us -> 10.7 us
    psum x4 -> x0, waiting for transfers between devices: 571 us -> none  [on_device(): grams = lax.psum(partial_grams, 'row')]
    all_to_all x0 -> x2, blocking collectives: none -> 43.1 us  [the longest x1 22.6 us: on_device(): lax.all_to_all(copies, 'row', split_axis=0, concat_axis=0, tiled=True)]
    dot_general x52 -> x0, matrix products: 18.5 us -> none  [the longest x20 6.95 us: rotation(): power = jnp.dot(power, term, precision=lax.Precision.HIGHEST) / float(order)]
    psum x4 -> x0, local copies, waits for them, and re-layouts: 14.9 us -> none  [on_device(): grams = lax.psum(partial_grams, 'row')]
    gather x9 -> x2, local copies, waits for them, and re-layouts: 12.9 us -> 1.57 us  [the longest x1 0.78 us: on_device(): other = jnp.take(arrived, order[PAIR:], axis=0)]
    pallas_call x0 -> x2, Pallas kernels: none -> 10.7 us  [the longest x1 9.37 us: on_device(): pl.pallas_call(rounds_kernel, out_shape=(pair, pair), in_specs=[scalar] +...]
    ppermute x6 -> x5, starting transfers between devices: 16.4 us -> 21.1 us  [passed(): lax.ppermute(value, 'col', [(source, where(source) % count) for source in...]
  transfers between devices with their start and end apart: 11 -> 6, of which waited for: 11 -> 4; matrix products, arithmetic and copies ran while one was open for 0% -> 1% of each run, Pallas kernels for 0% -> 0%
where the time goes in v2:
time: 120 us; the launch traced here: 119 us
  blocking collectives  43.1 us (36%)
  starting transfers between devices  38.4 us (32%)
  waiting for transfers between devices  23.9 us (20%)
  Pallas kernels  10.7 us (9%)
  local copies, waits for them, and re-layouts  2.01 us (2%)
  other arithmetic  1.23 us (1%)
    all_to_all x1, blocking collectives, on_device(): lax.all_to_all(copies, 'row', split_axis=0, concat_axis=0, tiled=True)  22.6 us
    ppermute x5, starting transfers between devices, passed(): lax.ppermute(value, 'col', [(source, where(source) % count) for source in...  21.1 us
    all_to_all x1, blocking collectives, on_device(): lax.all_to_all(parts, 'row', split_axis=0, concat_axis=0, tiled=True)  20.5 us
    all_to_all x1, starting transfers between devices, on_device(): lax.all_to_all(frames, 'row', split_axis=1, concat_axis=0, tiled=True)  17.3 us
    all_to_all x1, waiting for transfers between devices, on_device(): lax.all_to_all(frames, 'row', split_axis=1, concat_axis=0, tiled=True)  16.1 us
    pallas_call x1, Pallas kernels, on_device(): pl.pallas_call(rounds_kernel, out_shape=(pair, pair), in_specs=[scalar] +...  9.37 us
    ppermute x5, waiting for transfers between devices, passed(): lax.ppermute(value, 'col', [(source, where(source) % count) for source in...  7.86 us
  transfers between devices with their start and end apart: 6, of which 4 were waited for; matrix products, arithmetic and copies ran while one was open for 1% of the time, Pallas kernels for 0%

profile of v2, /device:TPU:1, one launch (start us, length us, event | category | flops | bytes accessed | tf_op | source)
XLA Modules:
  0.0 119.5 jit_solution(14978006837364330729)
XLA Ops:
  0.0 0.0 copy-start
  0.0 17.3 %all-to-all-start = ((bf16[3,64,1024]{2,0,1:T(4,128)(2,1)}), bf16[3,64,1024]{2,0,1:T(4,128)(2,1)S(1)}, u32[]{:S(2)}, u32[]{:S(2)}) async-start(bf16[3,64,1024]{2,0,1:T(4,128)(2,1)} %bitcast.8), calls=%async_computation | async-start | bytes 1048576 | tf_op jit(solution)/shard_map/all_to_all | solution.py:204
  17.3 0.0 copy-done
  17.3 0.1 fusion
  17.4 0.1 add_select_fusion
  17.4 0.1 compare_and_fusion
  17.5 16.1 %all-to-all-done = bf16[3,64,1024]{2,0,1:T(4,128)(2,1)S(1)} async-done(((bf16[3,64,1024]{2,0,1:T(4,128)(2,1)}), bf16[3,64,1024]{2,0,1:T(4,128)(2,1)S(1)}, u32[]{:S(2)}, u32[]{:S(2)}) %all-to-all-start) | async-done | bytes 393248 | tf_op jit(solution)/shard_map/all_to_all | solution.py:204
  33.6 0.3 all_to_all.23
  34.0 0.8 gather_fusion.1
  34.7 0.1 broadcast_select_fusion
  34.8 6.9 %collective-permute-start.1 = (bf16[96,1024]{1,0:T(8,128)(2,1)S(1)}, bf16[96,1024]{1,0:T(8,128)(2,1)S(1)}, u32[]{:S(2)}, u32[]{:S(2)}) collective-permute-start(bf16[96,1024]{1,0:T(8,128)(2,1)S(1)} %broadcast_select_fusion), channel_id=1, source_target_pairs={{0,448},{64,128},{128,64},{192,256},{256,192},{320,384},{384,320},... | collective-permute-start | bytes 589832 | tf_op jit(solution)/shard_map/ppermute | solution.py:197
  41.7 1.9 %collective-permute-start = (bf16[96,1024]{1,0:T(8,128)(2,1)S(1)}, bf16[96,1024]{1,0:T(8,128)(2,1)S(1)}, u32[]{:S(2)}, u32[]{:S(2)}) collective-permute-start(bf16[96,1024]{1,0:T(8,128)(2,1)S(1)} %broadcast_select_fusion), channel_id=1, source_target_pairs={{0,64},{64,0},{128,192},{192,128},{256,320},{320,256},{384,448},{4... | collective-permute-start | bytes 589832 | tf_op jit(solution)/shard_map/ppermute | solution.py:197
  43.7 0.8 gather_fusion
  44.4 0.1 broadcast_select_fusion.1.mine
  44.5 3.4 %collective-permute-start.3 = (bf16[96,1024]{1,0:T(8,128)(2,1)S(1)}, bf16[96,1024]{1,0:T(8,128)(2,1)S(1)}, u32[]{:S(2)}, u32[]{:S(2)}) collective-permute-start(bf16[96,1024]{1,0:T(8,128)(2,1)S(1)} %broadcast_select_fusion.1.mine), channel_id=1, source_target_pairs={{0,384},{64,448},{128,0},{192,64},{256,128},{320,192},{384,256},{4... | collective-permute-start | bytes 589832 | tf_op jit(solution)/shard_map/ppermute | solution.py:197
  47.9 1.9 %collective-permute-start.2 = (bf16[96,1024]{1,0:T(8,128)(2,1)S(1)}, bf16[96,1024]{1,0:T(8,128)(2,1)S(1)}, u32[]{:S(2)}, u32[]{:S(2)}) collective-permute-start(bf16[96,1024]{1,0:T(8,128)(2,1)S(1)} %broadcast_select_fusion.1.mine), channel_id=1, source_target_pairs={{0,128},{64,192},{128,256},{192,320},{256,384},{320,448},{384,0},{... | collective-permute-start | bytes 589832 | tf_op jit(solution)/shard_map/ppermute | solution.py:197
  49.8 0.0 collective-permute-done.1.across
  49.9 0.0 collective-permute-done.partner
  49.9 2.5 %collective-permute-done.3.right = bf16[96,1024]{1,0:T(8,128)(2,1)S(1)} collective-permute-done((bf16[96,1024]{1,0:T(8,128)(2,1)S(1)}, bf16[96,1024]{1,0:T(8,128)(2,1)S(1)}, u32[]{:S(2)}, u32[]{:S(2)}) %collective-permute-start.3) | collective-permute-done | bytes 196640 | tf_op jit(solution)/shard_map/ppermute | solution.py:197
  52.4 4.3 %collective-permute-done.2.left = bf16[96,1024]{1,0:T(8,128)(2,1)S(1)} collective-permute-done((bf16[96,1024]{1,0:T(8,128)(2,1)S(1)}, bf16[96,1024]{1,0:T(8,128)(2,1)S(1)}, u32[]{:S(2)}, u32[]{:S(2)}) %collective-permute-start.2) | collective-permute-done | bytes 196640 | tf_op jit(solution)/shard_map/ppermute | solution.py:197
  56.7 1.3 %grams.1 = f32[1024,128]{1,0:T(8,128)S(1)} custom-call(s32[1]{0:T(128)} %bitcast.core, bf16[96,1024]{1,0:T(8,128)(2,1)S(1)} %broadcast_select_fusion.1.mine, bf16[96,1024]{1,0:T(8,128)(2,1)S(1)} %collective-permute-done.partner, bf16[96,1024]{1,0:T(8,128)(2,1)S(1)} %collective-permute-done.1.across, bf16[96,1024]{1,0:T(8,128)(2,1)S(1)} %collective-permute-done.2.left, ...), custom_call_target="tpu_custom_call" | custom-call | tf_op jit(solution)/shard_map/grams/pallas_call | solution.py:219
  58.0 20.5 %all_to_all.29 = f32[64,16,128]{2,1,0:T(8,128)S(1)} all-to-all(f32[64,16,128]{2,1,0:T(8,128)S(1)} %bitcast.6), channel_id=1, replica_groups=mesh['col'=8,'row'=64] {'row'}, dimensions={0} | all-to-all | bytes 1048576 | tf_op jit(solution)/shard_map/all_to_all | solution.py:228
  78.5 0.1 reduce_sum.9
  78.7 22.6 %all_to_all.30 = f32[64,16,128]{2,1,0:T(8,128)S(1)} all-to-all(f32[64,16,128]{2,1,0:T(8,128)S(1)} %broadcast_in_dim.15), channel_id=1, replica_groups=mesh['col'=8,'row'=64] {'row'}, dimensions={0} | all-to-all | bytes 1048576 | tf_op jit(solution)/shard_map/all_to_all | solution.py:231
  101.2 9.4 %rounds.1 = (bf16[96,1024]{1,0:T(8,128)(2,1)S(1)}, bf16[96,1024]{1,0:T(8,128)(2,1)S(1)}) custom-call(s32[1]{0:T(128)} %bitcast.core, f32[1024,128]{1,0:T(8,128)S(1)} %bitcast.5, bf16[96,1024]{1,0:T(8,128)(2,1)S(1)} %broadcast_select_fusion.1.mine, bf16[96,1024]{1,0:T(8,128)(2,1)S(1)} %collective-permute-done.partner, ...), custom_call_target="tpu_custom_call" | custom-call | tf_op jit(solution)/shard_map/rounds/pallas_call | solution.py:233
  110.6 7.0 %collective-permute-start.4 = (bf16[96,1024]{1,0:T(8,128)(2,1)S(1)}, bf16[96,1024]{1,0:T(8,128)(2,1)S(1)}, u32[]{:S(2)}, u32[]{:S(2)}) collective-permute-start(bf16[96,1024]{1,0:T(8,128)(2,1)S(1)} %get-tuple-element.9), channel_id=1, source_target_pairs={{0,64},{64,0},{128,192},{192,128},{256,320},{320,256},{384,448},{4... | collective-permute-start | bytes 589832 | tf_op jit(solution)/shard_map/ppermute | solution.py:197
  117.6 1.0 collective-permute-done.4
  118.7 0.8 pad_maximum_fusion
  (4 shorter events, 0.1 us)
Async XLA Ops:
  0.0 17.3 %copy-start = (s32[192]{0:T(256)S(1)}, s32[192]{0:T(256)}, u32[]{:S(2)}) copy-start(s32[192]{0:T(256)} %param.5) | copy-start | bytes 2308
  0.0 33.6 %all-to-all-start = ((bf16[3,64,1024]{2,0,1:T(4,128)(2,1)}), bf16[3,64,1024]{2,0,1:T(4,128)(2,1)S(1)}, u32[]{:S(2)}, u32[]{:S(2)}) async-start(bf16[3,64,1024]{2,0,1:T(4,128)(2,1)} %bitcast.8), calls=%async_computation | async-start | bytes 1048576 | tf_op jit(solution)/shard_map/all_to_all | solution.py:204
  34.8 15.0 %collective-permute-start.1 = (bf16[96,1024]{1,0:T(8,128)(2,1)S(1)}, bf16[96,1024]{1,0:T(8,128)(2,1)S(1)}, u32[]{:S(2)}, u32[]{:S(2)}) collective-permute-start(bf16[96,1024]{1,0:T(8,128)(2,1)S(1)} %broadcast_select_fusion), channel_id=1, source_target_pairs={{0,448},{64,128},{128,64},{192,256},{256,192},{320,384},{384,320},... | collective-permute-start | bytes 589832 | tf_op jit(solution)/shard_map/ppermute | solution.py:197
  41.7 8.1 %collective-permute-start = (bf16[96,1024]{1,0:T(8,128)(2,1)S(1)}, bf16[96,1024]{1,0:T(8,128)(2,1)S(1)}, u32[]{:S(2)}, u32[]{:S(2)}) collective-permute-start(bf16[96,1024]{1,0:T(8,128)(2,1)S(1)} %broadcast_select_fusion), channel_id=1, source_target_pairs={{0,64},{64,0},{128,192},{192,128},{256,320},{320,256},{384,448},{4... | collective-permute-start | bytes 589832 | tf_op jit(solution)/shard_map/ppermute | solution.py:197
  44.5 7.9 %collective-permute-start.3 = (bf16[96,1024]{1,0:T(8,128)(2,1)S(1)}, bf16[96,1024]{1,0:T(8,128)(2,1)S(1)}, u32[]{:S(2)}, u32[]{:S(2)}) collective-permute-start(bf16[96,1024]{1,0:T(8,128)(2,1)S(1)} %broadcast_select_fusion.1.mine), channel_id=1, source_target_pairs={{0,384},{64,448},{128,0},{192,64},{256,128},{320,192},{384,256},{4... | collective-permute-start | bytes 589832 | tf_op jit(solution)/shard_map/ppermute | solution.py:197
  47.9 8.8 %collective-permute-start.2 = (bf16[96,1024]{1,0:T(8,128)(2,1)S(1)}, bf16[96,1024]{1,0:T(8,128)(2,1)S(1)}, u32[]{:S(2)}, u32[]{:S(2)}) collective-permute-start(bf16[96,1024]{1,0:T(8,128)(2,1)S(1)} %broadcast_select_fusion.1.mine), channel_id=1, source_target_pairs={{0,128},{64,192},{128,256},{192,320},{256,384},{320,448},{384,0},{... | collective-permute-start | bytes 589832 | tf_op jit(solution)/shard_map/ppermute | solution.py:197
  110.6 8.1 %collective-permute-start.4 = (bf16[96,1024]{1,0:T(8,128)(2,1)S(1)}, bf16[96,1024]{1,0:T(8,128)(2,1)S(1)}, u32[]{:S(2)}, u32[]{:S(2)}) collective-permute-start(bf16[96,1024]{1,0:T(8,128)(2,1)S(1)} %get-tuple-element.9), channel_id=1, source_target_pairs={{0,64},{64,0},{128,192},{192,128},{256,320},{320,256},{384,448},{4... | collective-permute-start | bytes 589832 | tf_op jit(solution)/shard_map/ppermute | solution.py:197

commit v3 on v2

--- a/solution.py
+++ b/solution.py
@@ -41,23 +41,23 @@
     return pltpu.roll(value, lanes % LANES, 1)
 
 
-def fill(rows_ref, core, mine, partner, across, left, right):
+def fill(rows_ref, core, mine, partner, near, far):
     first = core[0] == 0
     pieces = [
-        left[...],
-        jnp.where(first, across[...], partner[...]),
+        jnp.where(first, near[0:PAIR], far[...]),
+        jnp.where(first, near[PAIR:], partner[...]),
         mine[...],
-        jnp.where(first, partner[...], across[...]),
-        right[...],
+        jnp.where(first, partner[...], near[PAIR:]),
+        jnp.where(first, far[...], near[0:PAIR]),
     ]
     for s in range(SPAN):
         rows_ref[s, 0:PAIR, :] = pieces[s]
         rows_ref[s, PAIR:, :] = jnp.zeros((CHUNK, mine.shape[1]), jnp.bfloat16)
 
 
-def gram_kernel(core, mine, partner, across, left, right, packed, rows_ref):
+def gram_kernel(core, mine, partner, near, far, packed, rows_ref):
     width = mine.shape[1]
-    fill(rows_ref, core, mine, partner, across, left, right)
+    fill(rows_ref, core, mine, partner, near, far)
     block = {}
     for s in range(SPAN):
         end = min(s + ROUNDS, SPAN)
@@ -169,8 +169,8 @@
     return following
 
 
-def rounds_kernel(core, packed, mine, partner, across, left, right, kept, sent, rows_ref):
-    fill(rows_ref, core, mine, partner, across, left, right)
+def rounds_kernel(core, packed, mine, partner, near, far, out, sent, rows_ref):
+    fill(rows_ref, core, mine, partner, near, far)
     gram = unpacked(packed)
     for step in range(ROUNDS):
         count, reach = SPAN - step, ROUNDS - 1 - step
@@ -188,7 +188,7 @@
                 rows_ref[i, 0:BLOCK, :] = mm(upper, old).astype(jnp.bfloat16)
     first = core[0] == 0
     ends = [mm(turned[i][0:PAIR], rows_ref[i]).astype(jnp.bfloat16) for i in range(2)]
-    kept[...] = jnp.where(first, ends[0], ends[1])
+    out[pl.ds(pl.multiple_of(core[0] * PAIR, PAIR), PAIR), :] = jnp.where(first, ends[0], ends[1])
     sent[...] = jnp.where(first, ends[1], ends[0])
 
 
@@ -203,13 +203,13 @@
     core = lax.axis_index("col") % 2
     arrived = lax.all_to_all(frames, "row", split_axis=1, concat_axis=0, tiled=True)
     order = jnp.where(core == 0, jnp.roll(frame_order, PAIR), frame_order)
-    mine = jnp.take(arrived, order[:PAIR], axis=0)
-    other = jnp.take(arrived, order[PAIR:], axis=0)
+    picks = (order[:, None] == iota((1, order.shape[0]), 1)).astype(jnp.bfloat16)
+    mine = mm(picks[:PAIR], arrived).astype(jnp.bfloat16)
+    other = mm(picks[PAIR:], arrived).astype(jnp.bfloat16)
     partner = passed(other, lambda c: c ^ 1)
-    across = passed(other, lambda c: c - 1 if c % 2 == 0 else c + 1)
-    left = passed(mine, lambda c: c + 2)
-    right = passed(mine, lambda c: c - 2)
-    held = (mine, partner, across, left, right)
+    far = passed(mine, lambda c: c - 2 if c % 2 == 0 else c + 2)
+    near = passed(jnp.concatenate([mine, partner], axis=0), lambda c: c + 2 if c % 2 == 0 else c - 2)
+    held = (mine, partner, near, far)
     chosen = core.astype(jnp.int32).reshape(1)
     share = -(-USED // (8 * row_count)) * 8
     limit = pltpu.CompilerParams(vmem_limit_bytes=48 * 1024 * 1024)
@@ -219,7 +219,7 @@
     packed = pl.pallas_call(
         gram_kernel,
         out_shape=jax.ShapeDtypeStruct((share * row_count, LANES), jnp.float32),
-        in_specs=[scalar] + [vector] * 5,
+        in_specs=[scalar] + [vector] * 4,
         scratch_shapes=scratch,
         compiler_params=limit,
         name="grams",
@@ -229,19 +229,16 @@
     summed = jnp.sum(parts, axis=0)
     copies = jnp.broadcast_to(summed[None], (row_count, share, LANES))
     whole = lax.all_to_all(copies, "row", split_axis=0, concat_axis=0, tiled=True)
-    pair = jax.ShapeDtypeStruct((PAIR, width), jnp.bfloat16)
-    kept, sent = pl.pallas_call(
+    half, sent = pl.pallas_call(
         rounds_kernel,
-        out_shape=(pair, pair),
-        in_specs=[scalar] + [vector] * 6,
+        out_shape=tuple(jax.ShapeDtypeStruct((rows, width), jnp.bfloat16) for rows in (2 * PAIR, PAIR)),
+        in_specs=[scalar] + [vector] * 5,
         scratch_shapes=scratch,
         compiler_params=limit,
         name="rounds",
     )(chosen, whole.reshape(row_count * share, LANES), *held)
     got = passed(sent, lambda c: c ^ 1)
-    upper = jnp.where(core == 0, kept, got)
-    lower = jnp.where(core == 0, got, kept)
-    return jnp.concatenate([upper, lower], axis=0)
+    return lax.dynamic_update_slice(half, got, ((1 - core) * PAIR, 0))
 
 
 def solution(mesh):

time: 120 us -> 119 us (level)
  starting transfers between devices: 38.4 us -> 34.7 us
  blocking collectives: 43.1 us -> 45.7 us
    ppermute x5 -> x4, starting transfers between devices: 21.1 us -> 17.6 us  [passed(): lax.ppermute(value, 'col', [(source, where(source) % count) for source in...]
    all_to_all x1, blocking collectives: 20.5 us -> 23.4 us  [on_device(): lax.all_to_all(parts, 'row', split_axis=0, concat_axis=0, tiled=True)]
    gather x2 -> x0, local copies, waits for them, and re-layouts: 1.57 us -> none  [the longest x1 0.78 us: on_device(): other = jnp.take(arrived, order[PAIR:], axis=0)]
    ppermute x5 -> x4, waiting for transfers between devices: 7.86 us -> 8.22 us  [passed(): lax.ppermute(value, 'col', [(source, where(source) % count) for source in...]
  transfers between devices with their start and end apart: 6 -> 5, of which waited for: 4 -> 4; matrix products, arithmetic and copies ran while one was open for 1% -> 0% of each run, Pallas kernels for 0% -> 0%
where the time goes in v3:
time: 119 us; the launch traced here: 118 us
  blocking collectives  45.7 us (38%)
  starting transfers between devices  34.7 us (29%)
  waiting for transfers between devices  23.6 us (20%)
  Pallas kernels  11.4 us (10%)
  local copies, waits for them, and re-layouts  1.8 us (2%)
    all_to_all x1, blocking collectives, on_device(): lax.all_to_all(parts, 'row', split_axis=0, concat_axis=0, tiled=True)  23.4 us
    all_to_all x1, blocking collectives, on_device(): lax.all_to_all(copies, 'row', split_axis=0, concat_axis=0, tiled=True)  22.4 us
    ppermute x4, starting transfers between devices, passed(): lax.ppermute(value, 'col', [(source, where(source) % count) for source in...  17.6 us
    all_to_all x1, starting transfers between devices, on_device(): lax.all_to_all(frames, 'row', split_axis=1, concat_axis=0, tiled=True)  17.1 us
    all_to_all x1, waiting for transfers between devices, on_device(): lax.all_to_all(frames, 'row', split_axis=1, concat_axis=0, tiled=True)  15.4 us
    pallas_call x1, Pallas kernels, on_device(): pl.pallas_call(rounds_kernel, out_shape=tuple((jax.ShapeDtypeStruct((rows...  10.1 us
    ppermute x4, waiting for transfers between devices, passed(): lax.ppermute(value, 'col', [(source, where(source) % count) for source in...  8.22 us
  transfers between devices with their start and end apart: 5, of which 4 were waited for; matrix products, arithmetic and copies ran while one was open for 0% of the time, Pallas kernels for 0%

profile of v3, /device:TPU:1, one launch (start us, length us, event | category | flops | bytes accessed | tf_op | source)
XLA Modules:
  0.0 118.1 jit_solution(11251579924360915313)
XLA Ops:
  0.0 17.1 %all-to-all-start = ((bf16[3,64,1024]{2,0,1:T(4,128)(2,1)}), bf16[3,64,1024]{2,0,1:T(4,128)(2,1)S(1)}, u32[]{:S(2)}, u32[]{:S(2)}) async-start(bf16[3,64,1024]{2,0,1:T(4,128)(2,1)} %bitcast.10), calls=%async_computation | async-start | bytes 1048576 | tf_op jit(solution)/shard_map/all_to_all | solution.py:204
  17.2 0.0 copy-start
  17.2 0.7 copy-done
  17.8 0.1 fusion.2
  17.9 0.1 add_select_fusion
  18.0 0.1 iota_compare_fusion
  18.1 15.4 %all-to-all-done = bf16[3,64,1024]{2,0,1:T(4,128)(2,1)S(1)} async-done(((bf16[3,64,1024]{2,0,1:T(4,128)(2,1)}), bf16[3,64,1024]{2,0,1:T(4,128)(2,1)S(1)}, u32[]{:S(2)}, u32[]{:S(2)}) %all-to-all-start) | async-done | bytes 393248 | tf_op jit(solution)/shard_map/all_to_all | solution.py:204
  33.5 0.3 all_to_all.23
  33.8 0.2 convolution_convert_fusion
  34.0 5.8 %collective-permute-start = (bf16[96,1024]{1,0:T(8,128)(2,1)S(1)}, bf16[96,1024]{1,0:T(8,128)(2,1)S(1)}, u32[]{:S(2)}, u32[]{:S(2)}) collective-permute-start(bf16[96,1024]{1,0:T(8,128)(2,1)S(1)} %convolution_convert_fusion), channel_id=1, source_target_pairs={{0,64},{64,0},{128,192},{192,128},{256,320},{320,256},{384,448},{4... | collective-permute-start | bytes 589832 | tf_op jit(solution)/shard_map/ppermute | solution.py:197
  39.8 0.2 convolution_convert_fusion.1.mine
  40.1 0.8 collective-permute-done.partner
  40.9 4.4 %collective-permute-start.1 = (bf16[192,1024]{1,0:T(8,128)(2,1)S(1)}, bf16[192,1024]{1,0:T(8,128)(2,1)S(1)}, u32[]{:S(2)}, u32[]{:S(2)}) collective-permute-start(bf16[192,1024]{1,0:T(8,128)(2,1)S(1)} %pad_maximum_fusion), channel_id=1, source_target_pairs={{0,128},{64,448},{128,256},{192,64},{256,384},{320,192},{384,0},{4... | collective-permute-start | bytes 1179656 | tf_op jit(solution)/shard_map/ppermute | solution.py:197
  45.3 1.9 %collective-permute-start.2 = (bf16[96,1024]{1,0:T(8,128)(2,1)S(1)}, bf16[96,1024]{1,0:T(8,128)(2,1)S(1)}, u32[]{:S(2)}, u32[]{:S(2)}) collective-permute-start(bf16[96,1024]{1,0:T(8,128)(2,1)S(1)} %convolution_convert_fusion.1.mine), channel_id=1, source_target_pairs={{0,384},{64,192},{128,0},{192,320},{256,128},{320,448},{384,256},{... | collective-permute-start | bytes 589832 | tf_op jit(solution)/shard_map/ppermute | solution.py:197
  47.2 6.3 %collective-permute-done.2.far = bf16[96,1024]{1,0:T(8,128)(2,1)S(1)} collective-permute-done((bf16[96,1024]{1,0:T(8,128)(2,1)S(1)}, bf16[96,1024]{1,0:T(8,128)(2,1)S(1)}, u32[]{:S(2)}, u32[]{:S(2)}) %collective-permute-start.2) | collective-permute-done | bytes 196640 | tf_op jit(solution)/shard_map/ppermute | solution.py:197
  53.6 0.0 collective-permute-done.1.near
  53.6 1.3 %grams.1 = f32[1024,128]{1,0:T(8,128)S(1)} custom-call(s32[1]{0:T(128)} %bitcast.core, bf16[96,1024]{1,0:T(8,128)(2,1)S(1)} %convolution_convert_fusion.1.mine, bf16[96,1024]{1,0:T(8,128)(2,1)S(1)} %collective-permute-done.partner, bf16[192,1024]{1,0:T(8,128)(2,1)S(1)} %collective-permute-done.1.near, bf16[96,1024]{1,0:T(8,128)(2,1)S(1)} %collective-permute-done.2.far), custom_call_target="tpu_custom_call" | custom-call | tf_op jit(solution)/shard_map/grams/pallas_call | solution.py:219
  54.9 23.4 %all_to_all.29 = f32[64,16,128]{2,1,0:T(8,128)S(1)} all-to-all(f32[64,16,128]{2,1,0:T(8,128)S(1)} %bitcast.8), channel_id=1, replica_groups=mesh['col'=8,'row'=64] {'row'}, dimensions={0} | all-to-all | bytes 1048576 | tf_op jit(solution)/shard_map/all_to_all | solution.py:228
  78.3 0.1 reduce_sum.9
  78.4 22.4 %all_to_all.30 = f32[64,16,128]{2,1,0:T(8,128)S(1)} all-to-all(f32[64,16,128]{2,1,0:T(8,128)S(1)} %broadcast_in_dim.2), channel_id=1, replica_groups=mesh['col'=8,'row'=64] {'row'}, dimensions={0} | all-to-all | bytes 1048576 | tf_op jit(solution)/shard_map/all_to_all | solution.py:231
  100.8 10.1 %rounds.1 = (bf16[192,1024]{1,0:T(8,128)(2,1)}, bf16[96,1024]{1,0:T(8,128)(2,1)S(1)}) custom-call(s32[1]{0:T(128)} %bitcast.core, f32[1024,128]{1,0:T(8,128)S(1)} %bitcast.7, bf16[96,1024]{1,0:T(8,128)(2,1)S(1)} %convolution_convert_fusion.1.mine, bf16[96,1024]{1,0:T(8,128)(2,1)S(1)} %collective-permute-done.partner, ...), custom_call_target="tpu_custom_call" | custom-call | tf_op jit(solution)/shard_map/rounds/pallas_call | solution.py:232
  110.9 5.5 %collective-permute-start.3 = (bf16[96,1024]{1,0:T(8,128)(2,1)S(1)}, bf16[96,1024]{1,0:T(8,128)(2,1)S(1)}, u32[]{:S(2)}, u32[]{:S(2)}) collective-permute-start(bf16[96,1024]{1,0:T(8,128)(2,1)S(1)} %get-tuple-element.8), channel_id=1, source_target_pairs={{0,64},{64,0},{128,192},{192,128},{256,320},{320,256},{384,448},{4... | collective-permute-start | bytes 589832 | tf_op jit(solution)/shard_map/ppermute | solution.py:197
  116.4 1.0 collective-permute-done.3
  117.4 0.7 constant_dynamic-update-slice_fusion
  (2 shorter events, 0.1 us)
Async XLA Ops:
  0.0 33.5 %all-to-all-start = ((bf16[3,64,1024]{2,0,1:T(4,128)(2,1)}), bf16[3,64,1024]{2,0,1:T(4,128)(2,1)S(1)}, u32[]{:S(2)}, u32[]{:S(2)}) async-start(bf16[3,64,1024]{2,0,1:T(4,128)(2,1)} %bitcast.10), calls=%async_computation | async-start | bytes 1048576 | tf_op jit(solution)/shard_map/all_to_all | solution.py:204
  17.2 0.7 copy-start
  34.0 6.8 %collective-permute-start = (bf16[96,1024]{1,0:T(8,128)(2,1)S(1)}, bf16[96,1024]{1,0:T(8,128)(2,1)S(1)}, u32[]{:S(2)}, u32[]{:S(2)}) collective-permute-start(bf16[96,1024]{1,0:T(8,128)(2,1)S(1)} %convolution_convert_fusion), channel_id=1, source_target_pairs={{0,64},{64,0},{128,192},{192,128},{256,320},{320,256},{384,448},{4... | collective-permute-start | bytes 589832 | tf_op jit(solution)/shard_map/ppermute | solution.py:197
  40.9 12.7 %collective-permute-start.1 = (bf16[192,1024]{1,0:T(8,128)(2,1)S(1)}, bf16[192,1024]{1,0:T(8,128)(2,1)S(1)}, u32[]{:S(2)}, u32[]{:S(2)}) collective-permute-start(bf16[192,1024]{1,0:T(8,128)(2,1)S(1)} %pad_maximum_fusion), channel_id=1, source_target_pairs={{0,128},{64,448},{128,256},{192,64},{256,384},{320,192},{384,0},{4... | collective-permute-start | bytes 1179656 | tf_op jit(solution)/shard_map/ppermute | solution.py:197
  45.3 8.3 %collective-permute-start.2 = (bf16[96,1024]{1,0:T(8,128)(2,1)S(1)}, bf16[96,1024]{1,0:T(8,128)(2,1)S(1)}, u32[]{:S(2)}, u32[]{:S(2)}) collective-permute-start(bf16[96,1024]{1,0:T(8,128)(2,1)S(1)} %convolution_convert_fusion.1.mine), channel_id=1, source_target_pairs={{0,384},{64,192},{128,0},{192,320},{256,128},{320,448},{384,256},{... | collective-permute-start | bytes 589832 | tf_op jit(solution)/shard_map/ppermute | solution.py:197
  110.9 6.6 %collective-permute-start.3 = (bf16[96,1024]{1,0:T(8,128)(2,1)S(1)}, bf16[96,1024]{1,0:T(8,128)(2,1)S(1)}, u32[]{:S(2)}, u32[]{:S(2)}) collective-permute-start(bf16[96,1024]{1,0:T(8,128)(2,1)S(1)} %get-tuple-element.8), channel_id=1, source_target_pairs={{0,64},{64,0},{128,192},{192,128},{256,320},{320,256},{384,448},{4... | collective-permute-start | bytes 589832 | tf_op jit(solution)/shard_map/ppermute | solution.py:197

commit v4 on v3

--- a/solution.py
+++ b/solution.py
@@ -17,6 +17,7 @@
 SLOTS = 10
 CARRIERS, SPREAD, LAST = BLOCKS[:SLOTS], BLOCKS[SLOTS : SLOTS + 3], BLOCKS[SLOTS + 3]
 USED = SLOTS * PAIR + BLOCK
+EXTRA = 16
 
 
 def iota(shape, dim):
@@ -69,13 +70,23 @@
     last = block[LAST]
     for k in range(SLOTS):
         extra = shifted(block[SPREAD[k // 3]], PAIR - CHUNK * (k % 3)) if k < 9 else shifted(last, PAIR)
-        packed[k * PAIR : (k + 1) * PAIR, :] = jnp.where(lane < PAIR, block[CARRIERS[k]], extra)
-    packed[SLOTS * PAIR : USED, :] = jnp.where(
+        whole = jnp.where(lane < PAIR, block[CARRIERS[k]], extra)
+        packed[k * PAIR : (k + 1) * PAIR, :] = whole.astype(packed.dtype)
+    sides = jnp.where(
         lane[:BLOCK] < LANES // 2, shifted(last[:BLOCK], -CHUNK), shifted(last[BLOCK:], CHUNK)
     )
-    tail = packed.shape[0] - USED
+    packed[SLOTS * PAIR : USED, :] = sides.astype(packed.dtype)
+    place = iota((EXTRA, LANES), 0)
+    on_diagonal = iota((PAIR, LANES), 0) == lane
+    lost = jnp.zeros((EXTRA, LANES), jnp.float32)
+    for s in range(SPAN):
+        value = block[s, s]
+        gone = jnp.where(on_diagonal, value - value.astype(packed.dtype).astype(jnp.float32), 0.0)
+        lost = jnp.where(place == s, jnp.sum(gone, axis=0, keepdims=True), lost)
+    packed[USED : USED + EXTRA, :] = lost.astype(packed.dtype)
+    tail = packed.shape[0] - USED - EXTRA
     if tail:
-        packed[USED:, :] = jnp.zeros((tail, LANES), jnp.float32)
+        packed[USED + EXTRA :, :] = jnp.zeros((tail, LANES), packed.dtype)
 
 
 def unpacked(packed):
@@ -95,6 +106,9 @@
     sides = jnp.concatenate([shifted(rest, CHUNK), shifted(rest, -CHUNK)], axis=0)
     value = jnp.where(lane < CHUNK, shifted(slot[SLOTS - 1], -PAIR), sides)
     gram[LAST] = jnp.where(lane < PAIR, value, 0.0)
+    on_diagonal = iota((PAIR, LANES), 0) == lane
+    for s in range(SPAN):
+        gram[s, s] += jnp.where(on_diagonal, packed[USED + s : USED + s + 1, :], 0.0)
     return {name: jnp.concatenate([value, floor], axis=0) for name, value in gram.items()}
 
 
@@ -211,14 +225,14 @@
     near = passed(jnp.concatenate([mine, partner], axis=0), lambda c: c + 2 if c % 2 == 0 else c - 2)
     held = (mine, partner, near, far)
     chosen = core.astype(jnp.int32).reshape(1)
-    share = -(-USED // (8 * row_count)) * 8
+    share = -(-(USED + EXTRA) // (16 * row_count)) * 16
     limit = pltpu.CompilerParams(vmem_limit_bytes=48 * 1024 * 1024)
     scratch = [pltpu.VMEM((SPAN, LANES, width), jnp.bfloat16)]
     scalar = pl.BlockSpec(memory_space=pltpu.SMEM)
     vector = pl.BlockSpec(memory_space=pltpu.VMEM)
     packed = pl.pallas_call(
         gram_kernel,
-        out_shape=jax.ShapeDtypeStruct((share * row_count, LANES), jnp.float32),
+        out_shape=jax.ShapeDtypeStruct((share * row_count, LANES), jnp.bfloat16),
         in_specs=[scalar] + [vector] * 4,
         scratch_shapes=scratch,
         compiler_params=limit,
@@ -226,7 +240,7 @@
     )(chosen, *held)
     parts = packed.reshape(row_count, share, LANES)
     parts = lax.all_to_all(parts, "row", split_axis=0, concat_axis=0, tiled=True)
-    summed = jnp.sum(parts, axis=0)
+    summed = jnp.sum(parts.astype(jnp.float32), axis=0)
     copies = jnp.broadcast_to(summed[None], (row_count, share, LANES))
     whole = lax.all_to_all(copies, "row", split_axis=0, concat_axis=0, tiled=True)
     half, sent = pl.pallas_call(

time: 119 us -> 113 us (0.950)
  blocking collectives: 45.7 us -> 40.3 us
    all_to_all x1, blocking collectives: 23.4 us -> 19.1 us  [on_device(): lax.all_to_all(parts, 'row', split_axis=0, concat_axis=0, tiled=True)]
    all_to_all x1, blocking collectives: 22.4 us -> 21.1 us  [on_device(): lax.all_to_all(copies, 'row', split_axis=0, concat_axis=0, tiled=True)]
where the time goes in v4:
time: 113 us
  blocking collectives  40.3 us (36%)
  starting transfers between devices  34.6 us (31%)
  waiting for transfers between devices  23.6 us (21%)
  Pallas kernels  11.4 us (10%)
  local copies, waits for them, and re-layouts  1.8 us (2%)
    all_to_all x1, blocking collectives, on_device(): lax.all_to_all(copies, 'row', split_axis=0, concat_axis=0, tiled=True)  21.1 us
    all_to_all x1, blocking collectives, on_device(): lax.all_to_all(parts, 'row', split_axis=0, concat_axis=0, tiled=True)  19.1 us
    ppermute x4, starting transfers between devices, passed(): lax.ppermute(value, 'col', [(source, where(source) % count) for source in...  17.5 us
    all_to_all x1, starting transfers between devices, on_device(): lax.all_to_all(frames, 'row', split_axis=1, concat_axis=0, tiled=True)  17.1 us
    all_to_all x1, waiting for transfers between devices, on_device(): lax.all_to_all(frames, 'row', split_axis=1, concat_axis=0, tiled=True)  15.4 us
    pallas_call x1, Pallas kernels, on_device(): pl.pallas_call(rounds_kernel, out_shape=tuple((jax.ShapeDtypeStruct((rows...  10.1 us
    ppermute x4, waiting for transfers between devices, passed(): lax.ppermute(value, 'col', [(source, where(source) % count) for source in...  8.22 us
  transfers between devices with their start and end apart: 5, of which 4 were waited for; matrix products, arithmetic and copies ran while one was open for 0% of the time, Pallas kernels for 0%

profile of v4, /device:TPU:1, one launch (start us, length us, event | category | flops | bytes accessed | tf_op | source)
XLA Modules:
  0.0 112.5 jit_solution(14100500617094053604)
XLA Ops:
  0.0 17.1 %all-to-all-start = ((bf16[3,64,1024]{2,0,1:T(4,128)(2,1)}), bf16[3,64,1024]{2,0,1:T(4,128)(2,1)S(1)}, u32[]{:S(2)}, u32[]{:S(2)}) async-start(bf16[3,64,1024]{2,0,1:T(4,128)(2,1)} %bitcast.10), calls=%async_computation | async-start | bytes 1048576 | tf_op jit(solution)/shard_map/all_to_all | solution.py:218
  17.2 0.0 copy-start
  17.2 0.7 copy-done
  17.8 0.1 fusion.2
  17.9 0.1 add_select_fusion
  18.0 0.1 iota_compare_fusion
  18.1 15.4 %all-to-all-done = bf16[3,64,1024]{2,0,1:T(4,128)(2,1)S(1)} async-done(((bf16[3,64,1024]{2,0,1:T(4,128)(2,1)}), bf16[3,64,1024]{2,0,1:T(4,128)(2,1)S(1)}, u32[]{:S(2)}, u32[]{:S(2)}) %all-to-all-start) | async-done | bytes 393248 | tf_op jit(solution)/shard_map/all_to_all | solution.py:218
  33.5 0.3 all_to_all.23
  33.8 0.2 convolution_convert_fusion
  34.0 5.8 %collective-permute-start = (bf16[96,1024]{1,0:T(8,128)(2,1)S(1)}, bf16[96,1024]{1,0:T(8,128)(2,1)S(1)}, u32[]{:S(2)}, u32[]{:S(2)}) collective-permute-start(bf16[96,1024]{1,0:T(8,128)(2,1)S(1)} %convolution_convert_fusion), channel_id=1, source_target_pairs={{0,64},{64,0},{128,192},{192,128},{256,320},{320,256},{384,448},{4... | collective-permute-start | bytes 589832 | tf_op jit(solution)/shard_map/ppermute | solution.py:211
  39.8 0.2 convolution_convert_fusion.1.mine
  40.1 0.8 collective-permute-done.partner
  40.9 4.4 %collective-permute-start.1 = (bf16[192,1024]{1,0:T(8,128)(2,1)S(1)}, bf16[192,1024]{1,0:T(8,128)(2,1)S(1)}, u32[]{:S(2)}, u32[]{:S(2)}) collective-permute-start(bf16[192,1024]{1,0:T(8,128)(2,1)S(1)} %pad_maximum_fusion), channel_id=1, source_target_pairs={{0,128},{64,448},{128,256},{192,64},{256,384},{320,192},{384,0},{4... | collective-permute-start | bytes 1179656 | tf_op jit(solution)/shard_map/ppermute | solution.py:211
  45.3 1.9 %collective-permute-start.2 = (bf16[96,1024]{1,0:T(8,128)(2,1)S(1)}, bf16[96,1024]{1,0:T(8,128)(2,1)S(1)}, u32[]{:S(2)}, u32[]{:S(2)}) collective-permute-start(bf16[96,1024]{1,0:T(8,128)(2,1)S(1)} %convolution_convert_fusion.1.mine), channel_id=1, source_target_pairs={{0,384},{64,192},{128,0},{192,320},{256,128},{320,448},{384,256},{... | collective-permute-start | bytes 589832 | tf_op jit(solution)/shard_map/ppermute | solution.py:211
  47.2 6.3 %collective-permute-done.2.far = bf16[96,1024]{1,0:T(8,128)(2,1)S(1)} collective-permute-done((bf16[96,1024]{1,0:T(8,128)(2,1)S(1)}, bf16[96,1024]{1,0:T(8,128)(2,1)S(1)}, u32[]{:S(2)}, u32[]{:S(2)}) %collective-permute-start.2) | collective-permute-done | bytes 196640 | tf_op jit(solution)/shard_map/ppermute | solution.py:211
  53.6 0.0 collective-permute-done.1.near
  53.6 1.3 %grams.1 = bf16[1024,128]{1,0:T(8,128)(2,1)S(1)} custom-call(s32[1]{0:T(128)} %bitcast.core, bf16[96,1024]{1,0:T(8,128)(2,1)S(1)} %convolution_convert_fusion.1.mine, bf16[96,1024]{1,0:T(8,128)(2,1)S(1)} %collective-permute-done.partner, bf16[192,1024]{1,0:T(8,128)(2,1)S(1)} %collective-permute-done.1.near, bf16[96,1024]{1,0:T(8,128)(2,1)S(1)} %collective-permute-done.2.far), custom_call_target="tpu_custom_call" | custom-call | tf_op jit(solution)/shard_map/grams/pallas_call | solution.py:233
  54.9 19.1 %all_to_all.29 = bf16[64,16,128]{2,1,0:T(8,128)(2,1)S(1)} all-to-all(bf16[64,16,128]{2,1,0:T(8,128)(2,1)S(1)} %bitcast.8), channel_id=1, replica_groups=mesh['col'=8,'row'=64] {'row'}, dimensions={0} | all-to-all | bytes 524288 | tf_op jit(solution)/shard_map/all_to_all | solution.py:242
  74.0 0.1 convert_reduce_fusion
  74.1 21.1 %all_to_all.30 = f32[64,16,128]{2,1,0:T(8,128)S(1)} all-to-all(f32[64,16,128]{2,1,0:T(8,128)S(1)} %broadcast_in_dim.2), channel_id=1, replica_groups=mesh['col'=8,'row'=64] {'row'}, dimensions={0} | all-to-all | bytes 1048576 | tf_op jit(solution)/shard_map/all_to_all | solution.py:245
  95.3 10.1 %rounds.1 = (bf16[192,1024]{1,0:T(8,128)(2,1)}, bf16[96,1024]{1,0:T(8,128)(2,1)S(1)}) custom-call(s32[1]{0:T(128)} %bitcast.core, f32[1024,128]{1,0:T(8,128)S(1)} %bitcast.7, bf16[96,1024]{1,0:T(8,128)(2,1)S(1)} %convolution_convert_fusion.1.mine, bf16[96,1024]{1,0:T(8,128)(2,1)S(1)} %collective-permute-done.partner, ...), custom_call_target="tpu_custom_call" | custom-call | tf_op jit(solution)/shard_map/rounds/pallas_call | solution.py:246
  105.4 5.4 %collective-permute-start.3 = (bf16[96,1024]{1,0:T(8,128)(2,1)S(1)}, bf16[96,1024]{1,0:T(8,128)(2,1)S(1)}, u32[]{:S(2)}, u32[]{:S(2)}) collective-permute-start(bf16[96,1024]{1,0:T(8,128)(2,1)S(1)} %get-tuple-element.8), channel_id=1, source_target_pairs={{0,64},{64,0},{128,192},{192,128},{256,320},{320,256},{384,448},{4... | collective-permute-start | bytes 589832 | tf_op jit(solution)/shard_map/ppermute | solution.py:211
  110.8 1.0 collective-permute-done.3
  111.8 0.7 constant_dynamic-update-slice_fusion
  (2 shorter events, 0.1 us)
Async XLA Ops:
  0.0 33.5 %all-to-all-start = ((bf16[3,64,1024]{2,0,1:T(4,128)(2,1)}), bf16[3,64,1024]{2,0,1:T(4,128)(2,1)S(1)}, u32[]{:S(2)}, u32[]{:S(2)}) async-start(bf16[3,64,1024]{2,0,1:T(4,128)(2,1)} %bitcast.10), calls=%async_computation | async-start | bytes 1048576 | tf_op jit(solution)/shard_map/all_to_all | solution.py:218
  17.2 0.7 copy-start
  34.0 6.8 %collective-permute-start = (bf16[96,1024]{1,0:T(8,128)(2,1)S(1)}, bf16[96,1024]{1,0:T(8,128)(2,1)S(1)}, u32[]{:S(2)}, u32[]{:S(2)}) collective-permute-start(bf16[96,1024]{1,0:T(8,128)(2,1)S(1)} %convolution_convert_fusion), channel_id=1, source_target_pairs={{0,64},{64,0},{128,192},{192,128},{256,320},{320,256},{384,448},{4... | collective-permute-start | bytes 589832 | tf_op jit(solution)/shard_map/ppermute | solution.py:211
  40.9 12.7 %collective-permute-start.1 = (bf16[192,1024]{1,0:T(8,128)(2,1)S(1)}, bf16[192,1024]{1,0:T(8,128)(2,1)S(1)}, u32[]{:S(2)}, u32[]{:S(2)}) collective-permute-start(bf16[192,1024]{1,0:T(8,128)(2,1)S(1)} %pad_maximum_fusion), channel_id=1, source_target_pairs={{0,128},{64,448},{128,256},{192,64},{256,384},{320,192},{384,0},{4... | collective-permute-start | bytes 1179656 | tf_op jit(solution)/shard_map/ppermute | solution.py:211
  45.3 8.3 %collective-permute-start.2 = (bf16[96,1024]{1,0:T(8,128)(2,1)S(1)}, bf16[96,1024]{1,0:T(8,128)(2,1)S(1)}, u32[]{:S(2)}, u32[]{:S(2)}) collective-permute-start(bf16[96,1024]{1,0:T(8,128)(2,1)S(1)} %convolution_convert_fusion.1.mine), channel_id=1, source_target_pairs={{0,384},{64,192},{128,0},{192,320},{256,128},{320,448},{384,256},{... | collective-permute-start | bytes 589832 | tf_op jit(solution)/shard_map/ppermute | solution.py:211
  105.4 6.4 %collective-permute-start.3 = (bf16[96,1024]{1,0:T(8,128)(2,1)S(1)}, bf16[96,1024]{1,0:T(8,128)(2,1)S(1)}, u32[]{:S(2)}, u32[]{:S(2)}) collective-permute-start(bf16[96,1024]{1,0:T(8,128)(2,1)S(1)} %get-tuple-element.8), channel_id=1, source_target_pairs={{0,64},{64,0},{128,192},{192,128},{256,320},{320,256},{384,448},{4... | collective-permute-start | bytes 589832 | tf_op jit(solution)/shard_map/ppermute | solution.py:211

commit v5 on v4

--- a/solution.py
+++ b/solution.py
@@ -113,10 +113,9 @@
 
 
 def product(a, b):
-    ah, al = a
-    bh, bl = b
-    wide = mm(jnp.concatenate([ah, al], axis=0), jnp.concatenate([bh, bl], axis=1))
-    return wide[:LANES, :LANES] + (wide[LANES:, :LANES] + wide[:LANES, LANES:])
+    (ah, al), (bh, bl) = a, b
+    value = mm(ah[:PAIR], bh) + (mm(al[:PAIR], bh) + mm(ah[:PAIR], bl))
+    return jnp.concatenate([value, jnp.zeros((CHUNK, LANES), jnp.float32)], axis=0)
 
 
 def turned_rotors(grams):
@@ -183,9 +182,22 @@
     return following
 
 
-def rounds_kernel(core, packed, mine, partner, near, far, out, sent, rows_ref):
-    fill(rows_ref, core, mine, partner, near, far)
+def turn(rows, turned, i, into):
+    old = rows[i]
+    value = mm(turned[i][0:PAIR], old).astype(jnp.bfloat16)
+    if i > 0:
+        into[i - 1, BLOCK:PAIR, :] = value[BLOCK:]
+    if i < into.shape[0]:
+        into[i, 0:BLOCK, :] = value[:BLOCK]
+
+
+def rounds_kernel(core, packed, rows_ref, kept, sent, *later):
+    width = kept.shape[1]
+    for ref in later:
+        for i in range(ref.shape[0]):
+            ref[i, PAIR:, :] = jnp.zeros((CHUNK, width), jnp.bfloat16)
     gram = unpacked(packed)
+    rows = rows_ref
     for step in range(ROUNDS):
         count, reach = SPAN - step, ROUNDS - 1 - step
         turned = turned_rotors([gram[s, s] for s in range(count)])
@@ -193,16 +205,11 @@
             break
         gram = next_grams(gram, turned, count, reach)
         for i in range(count):
-            old = rows_ref[i]
-            if i > 0:
-                lower = turned[i][BLOCK:PAIR]
-                rows_ref[i - 1, BLOCK:PAIR, :] = mm(lower, old).astype(jnp.bfloat16)
-            if i < count - 1:
-                upper = turned[i][0:BLOCK]
-                rows_ref[i, 0:BLOCK, :] = mm(upper, old).astype(jnp.bfloat16)
+            turn(rows, turned, i, later[step])
+        rows = later[step]
     first = core[0] == 0
-    ends = [mm(turned[i][0:PAIR], rows_ref[i]).astype(jnp.bfloat16) for i in range(2)]
-    out[pl.ds(pl.multiple_of(core[0] * PAIR, PAIR), PAIR), :] = jnp.where(first, ends[0], ends[1])
+    ends = [mm(turned[i][0:PAIR], rows[i]).astype(jnp.bfloat16) for i in range(2)]
+    kept[...] = jnp.where(first, ends[0], ends[1])
     sent[...] = jnp.where(first, ends[1], ends[0])
 
 
@@ -227,14 +234,16 @@
     chosen = core.astype(jnp.int32).reshape(1)
     share = -(-(USED + EXTRA) // (16 * row_count)) * 16
     limit = pltpu.CompilerParams(vmem_limit_bytes=48 * 1024 * 1024)
-    scratch = [pltpu.VMEM((SPAN, LANES, width), jnp.bfloat16)]
     scalar = pl.BlockSpec(memory_space=pltpu.SMEM)
     vector = pl.BlockSpec(memory_space=pltpu.VMEM)
-    packed = pl.pallas_call(
+    packed, rows = pl.pallas_call(
         gram_kernel,
-        out_shape=jax.ShapeDtypeStruct((share * row_count, LANES), jnp.bfloat16),
+        out_shape=(
+            jax.ShapeDtypeStruct((share * row_count, LANES), jnp.bfloat16),
+            jax.ShapeDtypeStruct((SPAN, LANES, width), jnp.bfloat16),
+        ),
         in_specs=[scalar] + [vector] * 4,
-        scratch_shapes=scratch,
+        out_specs=(vector, vector),
         compiler_params=limit,
         name="grams",
     )(chosen, *held)
@@ -243,16 +252,18 @@
     summed = jnp.sum(parts.astype(jnp.float32), axis=0)
     copies = jnp.broadcast_to(summed[None], (row_count, share, LANES))
     whole = lax.all_to_all(copies, "row", split_axis=0, concat_axis=0, tiled=True)
-    half, sent = pl.pallas_call(
+    pair = jax.ShapeDtypeStruct((PAIR, width), jnp.bfloat16)
+    kept, sent = pl.pallas_call(
         rounds_kernel,
-        out_shape=tuple(jax.ShapeDtypeStruct((rows, width), jnp.bfloat16) for rows in (2 * PAIR, PAIR)),
-        in_specs=[scalar] + [vector] * 5,
-        scratch_shapes=scratch,
+        out_shape=(pair, pair),
+        in_specs=[scalar, vector, vector],
+        out_specs=(vector, vector),
+        scratch_shapes=[pltpu.VMEM((SPAN - 1 - step, LANES, width), jnp.bfloat16) for step in range(ROUNDS - 1)],
         compiler_params=limit,
         name="rounds",
-    )(chosen, whole.reshape(row_count * share, LANES), *held)
+    )(chosen, whole.reshape(row_count * share, LANES), rows)
     got = passed(sent, lambda c: c ^ 1)
-    return lax.dynamic_update_slice(half, got, ((1 - core) * PAIR, 0))
+    return jnp.concatenate([jnp.where(core == 0, kept, got), jnp.where(core == 0, got, kept)], axis=0)
 
 
 def solution(mesh):

time: 113 us -> 112 us (level)
  other arithmetic: 0.27 us -> 1.75 us
    pallas_call x2, Pallas kernels: 11.4 us -> 10.3 us  [the longest x1 8.91 us: on_device(): pl.pallas_call(rounds_kernel, out_shape=(pair, pair), in_specs=[scalar, v...]
  transfers between devices with their start and end apart: 5 -> 5, of which waited for: 4 -> 4; matrix products, arithmetic and copies ran while one was open for 0% -> 2% of each run, Pallas kernels for 0% -> 0%
where the time goes in v5:
time: 112 us; the launch traced here: 111 us
  blocking collectives  40.2 us (36%)
  starting transfers between devices  34.6 us (31%)
  waiting for transfers between devices  22.9 us (20%)
  Pallas kernels  10.3 us (9%)
  other arithmetic  1.75 us (2%)
  local copies, waits for them, and re-layouts  1.19 us (1%)
    all_to_all x1, blocking collectives, on_device(): lax.all_to_all(copies, 'row', split_axis=0, concat_axis=0, tiled=True)  21.1 us
    all_to_all x1, blocking collectives, on_device(): lax.all_to_all(parts, 'row', split_axis=0, concat_axis=0, tiled=True)  19.1 us
    ppermute x4, starting transfers between devices, passed(): lax.ppermute(value, 'col', [(source, where(source) % count) for source in...  17.5 us
    all_to_all x1, starting transfers between devices, on_device(): lax.all_to_all(frames, 'row', split_axis=1, concat_axis=0, tiled=True)  17.1 us
    all_to_all x1, waiting for transfers between devices, on_device(): lax.all_to_all(frames, 'row', split_axis=1, concat_axis=0, tiled=True)  14.6 us
    pallas_call x1, Pallas kernels, on_device(): pl.pallas_call(rounds_kernel, out_shape=(pair, pair), in_specs=[scalar, v...  8.91 us
    ppermute x4, waiting for transfers between devices, passed(): lax.ppermute(value, 'col', [(source, where(source) % count) for source in...  8.23 us
  transfers between devices with their start and end apart: 5, of which 4 were waited for; matrix products, arithmetic and copies ran while one was open for 2% of the time, Pallas kernels for 0%

profile of v5, /device:TPU:1, one launch (start us, length us, event | category | flops | bytes accessed | tf_op | source)
XLA Modules:
  0.0 111.5 jit_solution(2543272664722442029)
XLA Ops:
  0.0 17.1 %all-to-all-start = ((bf16[3,64,1024]{2,0,1:T(4,128)(2,1)}), bf16[3,64,1024]{2,0,1:T(4,128)(2,1)S(1)}, u32[]{:S(2)}, u32[]{:S(2)}) async-start(bf16[3,64,1024]{2,0,1:T(4,128)(2,1)} %bitcast.10), calls=%async_computation | async-start | bytes 1048576 | tf_op jit(solution)/shard_map/all_to_all | solution.py:225
  17.2 0.8 fusion.2
  18.0 0.8 add_select_fusion
  18.7 0.1 iota_compare_fusion
  18.8 14.6 %all-to-all-done = bf16[3,64,1024]{2,0,1:T(4,128)(2,1)S(1)} async-done(((bf16[3,64,1024]{2,0,1:T(4,128)(2,1)}), bf16[3,64,1024]{2,0,1:T(4,128)(2,1)S(1)}, u32[]{:S(2)}, u32[]{:S(2)}) %all-to-all-start) | async-done | bytes 393248 | tf_op jit(solution)/shard_map/all_to_all | solution.py:225
  33.5 0.3 all_to_all.23
  33.8 0.2 convolution_convert_fusion
  34.0 5.8 %collective-permute-start = (bf16[96,1024]{1,0:T(8,128)(2,1)S(1)}, bf16[96,1024]{1,0:T(8,128)(2,1)S(1)}, u32[]{:S(2)}, u32[]{:S(2)}) collective-permute-start(bf16[96,1024]{1,0:T(8,128)(2,1)S(1)} %convolution_convert_fusion), channel_id=1, source_target_pairs={{0,64},{64,0},{128,192},{192,128},{256,320},{320,256},{384,448},{4... | collective-permute-start | bytes 589832 | tf_op jit(solution)/shard_map/ppermute | solution.py:218
  39.8 0.2 convolution_convert_fusion.1.mine
  40.1 0.8 collective-permute-done.partner
  40.9 4.4 %collective-permute-start.1 = (bf16[192,1024]{1,0:T(8,128)(2,1)S(1)}, bf16[192,1024]{1,0:T(8,128)(2,1)S(1)}, u32[]{:S(2)}, u32[]{:S(2)}) collective-permute-start(bf16[192,1024]{1,0:T(8,128)(2,1)S(1)} %pad_maximum_fusion), channel_id=1, source_target_pairs={{0,128},{64,448},{128,256},{192,64},{256,384},{320,192},{384,0},{4... | collective-permute-start | bytes 1179656 | tf_op jit(solution)/shard_map/ppermute | solution.py:218
  45.3 1.9 %collective-permute-start.2 = (bf16[96,1024]{1,0:T(8,128)(2,1)S(1)}, bf16[96,1024]{1,0:T(8,128)(2,1)S(1)}, u32[]{:S(2)}, u32[]{:S(2)}) collective-permute-start(bf16[96,1024]{1,0:T(8,128)(2,1)S(1)} %convolution_convert_fusion.1.mine), channel_id=1, source_target_pairs={{0,384},{64,192},{128,0},{192,320},{256,128},{320,448},{384,256},{... | collective-permute-start | bytes 589832 | tf_op jit(solution)/shard_map/ppermute | solution.py:218
  47.2 6.3 %collective-permute-done.2.far = bf16[96,1024]{1,0:T(8,128)(2,1)S(1)} collective-permute-done((bf16[96,1024]{1,0:T(8,128)(2,1)S(1)}, bf16[96,1024]{1,0:T(8,128)(2,1)S(1)}, u32[]{:S(2)}, u32[]{:S(2)}) %collective-permute-start.2) | collective-permute-done | bytes 196640 | tf_op jit(solution)/shard_map/ppermute | solution.py:218
  53.6 0.0 collective-permute-done.1.near
  53.6 1.3 %grams.1 = (bf16[1024,128]{1,0:T(8,128)(2,1)S(1)}, bf16[5,128,1024]{2,1,0:T(8,128)(2,1)S(1)}) custom-call(s32[1]{0:T(128)} %bitcast.core, bf16[96,1024]{1,0:T(8,128)(2,1)S(1)} %convolution_convert_fusion.1.mine, bf16[96,1024]{1,0:T(8,128)(2,1)S(1)} %collective-permute-done.partner, bf16[192,1024]{1,0:T(8,128)(2,1)S(1)} %collective-permute-done.1.near, ...), custom_call_target="tpu_custom_call" | custom-call | tf_op jit(solution)/shard_map/grams/pallas_call | solution.py:239
  54.9 19.1 %all_to_all.29 = bf16[64,16,128]{2,1,0:T(8,128)(2,1)S(1)} all-to-all(bf16[64,16,128]{2,1,0:T(8,128)(2,1)S(1)} %bitcast.8), channel_id=1, replica_groups=mesh['col'=8,'row'=64] {'row'}, dimensions={0} | all-to-all | bytes 524288 | tf_op jit(solution)/shard_map/all_to_all | solution.py:251
  74.1 0.1 convert_reduce_fusion
  74.2 21.1 %all_to_all.30 = f32[64,16,128]{2,1,0:T(8,128)S(1)} all-to-all(f32[64,16,128]{2,1,0:T(8,128)S(1)} %broadcast_in_dim.2), channel_id=1, replica_groups=mesh['col'=8,'row'=64] {'row'}, dimensions={0} | all-to-all | bytes 1048576 | tf_op jit(solution)/shard_map/all_to_all | solution.py:254
  95.3 8.9 %rounds.1 = (bf16[96,1024]{1,0:T(8,128)(2,1)S(1)}, bf16[96,1024]{1,0:T(8,128)(2,1)S(1)}) custom-call(s32[1]{0:T(128)} %bitcast.core, f32[1024,128]{1,0:T(8,128)S(1)} %bitcast.7, bf16[5,128,1024]{2,1,0:T(8,128)(2,1)S(1)} %get-tuple-element.10.rows_ref), custom_call_target="tpu_custom_call" | custom-call | tf_op jit(solution)/shard_map/rounds/pallas_call | solution.py:256
  104.2 5.4 %collective-permute-start.3 = (bf16[96,1024]{1,0:T(8,128)(2,1)S(1)}, bf16[96,1024]{1,0:T(8,128)(2,1)S(1)}, u32[]{:S(2)}, u32[]{:S(2)}) collective-permute-start(bf16[96,1024]{1,0:T(8,128)(2,1)S(1)} %get-tuple-element.12), channel_id=1, source_target_pairs={{0,64},{64,0},{128,192},{192,128},{256,320},{320,256},{384,448},{4... | collective-permute-start | bytes 589832 | tf_op jit(solution)/shard_map/ppermute | solution.py:218
  109.6 1.0 collective-permute-done.3
  110.7 0.8 pad_maximum_fusion.1
  (3 shorter events, 0.1 us)
Async XLA Ops:
  0.0 33.5 %all-to-all-start = ((bf16[3,64,1024]{2,0,1:T(4,128)(2,1)}), bf16[3,64,1024]{2,0,1:T(4,128)(2,1)S(1)}, u32[]{:S(2)}, u32[]{:S(2)}) async-start(bf16[3,64,1024]{2,0,1:T(4,128)(2,1)} %bitcast.10), calls=%async_computation | async-start | bytes 1048576 | tf_op jit(solution)/shard_map/all_to_all | solution.py:225
  34.0 6.8 %collective-permute-start = (bf16[96,1024]{1,0:T(8,128)(2,1)S(1)}, bf16[96,1024]{1,0:T(8,128)(2,1)S(1)}, u32[]{:S(2)}, u32[]{:S(2)}) collective-permute-start(bf16[96,1024]{1,0:T(8,128)(2,1)S(1)} %convolution_convert_fusion), channel_id=1, source_target_pairs={{0,64},{64,0},{128,192},{192,128},{256,320},{320,256},{384,448},{4... | collective-permute-start | bytes 589832 | tf_op jit(solution)/shard_map/ppermute | solution.py:218
  40.9 12.7 %collective-permute-start.1 = (bf16[192,1024]{1,0:T(8,128)(2,1)S(1)}, bf16[192,1024]{1,0:T(8,128)(2,1)S(1)}, u32[]{:S(2)}, u32[]{:S(2)}) collective-permute-start(bf16[192,1024]{1,0:T(8,128)(2,1)S(1)} %pad_maximum_fusion), channel_id=1, source_target_pairs={{0,128},{64,448},{128,256},{192,64},{256,384},{320,192},{384,0},{4... | collective-permute-start | bytes 1179656 | tf_op jit(solution)/shard_map/ppermute | solution.py:218
  45.3 8.3 %collective-permute-start.2 = (bf16[96,1024]{1,0:T(8,128)(2,1)S(1)}, bf16[96,1024]{1,0:T(8,128)(2,1)S(1)}, u32[]{:S(2)}, u32[]{:S(2)}) collective-permute-start(bf16[96,1024]{1,0:T(8,128)(2,1)S(1)} %convolution_convert_fusion.1.mine), channel_id=1, source_target_pairs={{0,384},{64,192},{128,0},{192,320},{256,128},{320,448},{384,256},{... | collective-permute-start | bytes 589832 | tf_op jit(solution)/shard_map/ppermute | solution.py:218
  104.2 6.4 %collective-permute-start.3 = (bf16[96,1024]{1,0:T(8,128)(2,1)S(1)}, bf16[96,1024]{1,0:T(8,128)(2,1)S(1)}, u32[]{:S(2)}, u32[]{:S(2)}) collective-permute-start(bf16[96,1024]{1,0:T(8,128)(2,1)S(1)} %get-tuple-element.12), channel_id=1, source_target_pairs={{0,64},{64,0},{128,192},{192,128},{256,320},{320,256},{384,448},{4... | collective-permute-start | bytes 589832 | tf_op jit(solution)/shard_map/ppermute | solution.py:218

commit v6 on v5

--- a/solution.py
+++ b/solution.py
@@ -222,7 +222,11 @@
     row_count = lax.axis_size("row")
     width = frames.shape[1] // row_count
     core = lax.axis_index("col") % 2
-    arrived = lax.all_to_all(frames, "row", split_axis=1, concat_axis=0, tiled=True)
+    deep = width // LANES
+    tiles = frames.reshape(-1, row_count, deep, LANES).transpose(1, 0, 2, 3)
+    tiles = tiles.reshape(row_count, -1, LANES)
+    arrived = lax.all_to_all(tiles, "row", split_axis=0, concat_axis=0, tiled=True)
+    arrived = arrived.reshape(frame_order.shape[0], width)
     order = jnp.where(core == 0, jnp.roll(frame_order, PAIR), frame_order)
     picks = (order[:, None] == iota((1, order.shape[0]), 1)).astype(jnp.bfloat16)
     mine = mm(picks[:PAIR], arrived).astype(jnp.bfloat16)

time: 112 us -> 111 us (level)
    reshape x0 -> x2, local copies, waits for them, and re-layouts: none -> 2.03 us  [the longest x1 1.86 us: on_device(): tiles = tiles.reshape(row_count, -1, LANES)]
  transfers between devices with their start and end apart: 5 -> 5, of which waited for: 4 -> 4; matrix products, arithmetic and copies ran while one was open for 2% -> 0% of each run, Pallas kernels for 0% -> 0%
where the time goes in v6:
time: 111 us; the launch traced here: 110 us
  blocking collectives  39.7 us (36%)
  starting transfers between devices  34.1 us (31%)
  waiting for transfers between devices  22.6 us (20%)
  Pallas kernels  10.3 us (9%)
  local copies, waits for them, and re-layouts  2.14 us (2%)
    all_to_all x1, blocking collectives, on_device(): lax.all_to_all(copies, 'row', split_axis=0, concat_axis=0, tiled=True)  21.1 us
    all_to_all x1, blocking collectives, on_device(): lax.all_to_all(parts, 'row', split_axis=0, concat_axis=0, tiled=True)  18.5 us
    all_to_all x1, starting transfers between devices, on_device(): lax.all_to_all(tiles, 'row', split_axis=0, concat_axis=0, tiled=True)  17.1 us
    ppermute x4, starting transfers between devices, passed(): lax.ppermute(value, 'col', [(source, where(source) % count) for source in...  16.9 us
    all_to_all x1, waiting for transfers between devices, on_device(): lax.all_to_all(tiles, 'row', split_axis=0, concat_axis=0, tiled=True)  14.4 us
    pallas_call x1, Pallas kernels, on_device(): pl.pallas_call(rounds_kernel, out_shape=(pair, pair), in_specs=[scalar, v...  8.91 us
    ppermute x4, waiting for transfers between devices, passed(): lax.ppermute(value, 'col', [(source, where(source) % count) for source in...  8.23 us
  transfers between devices with their start and end apart: 5, of which 4 were waited for; matrix products, arithmetic and copies ran while one was open for 0% of the time, Pallas kernels for 0%

profile of v6, /device:TPU:1, one launch (start us, length us, event | category | flops | bytes accessed | tf_op | source)
XLA Modules:
  0.0 110.4 jit_solution(16715840235136875783)
XLA Ops:
  0.0 0.0 copy-start
  0.0 1.9 %copy_bitcast_fusion = bf16[64,24,128]{2,1,0:T(8,128)(2,1)} fusion(bf16[1,3,512,128]{3,1,2,0:T(4,128)(2,1)} %bitcast.17), kind=kLoop, calls=%fused_computation.6 | loop fusion | bytes 786432 | tf_op jit(solution)/shard_map/reshape | solution.py:227
  1.9 17.1 %all-to-all-start = ((bf16[64,24,128]{2,1,0:T(8,128)(2,1)}), bf16[64,24,128]{2,1,0:T(8,128)(2,1)S(1)}, u32[]{:S(2)}, u32[]{:S(2)}) async-start(bf16[64,24,128]{2,1,0:T(8,128)(2,1)} %copy_bitcast_fusion), calls=%async_computation | async-start | bytes 786432 | tf_op jit(solution)/shard_map/all_to_all | solution.py:228
  19.0 0.0 copy-done
  19.0 0.1 fusion.2
  19.1 0.1 add_select_fusion
  19.2 0.1 iota_compare_fusion
  19.3 14.4 %all-to-all-done = bf16[64,24,128]{2,1,0:T(8,128)(2,1)S(1)} async-done(((bf16[64,24,128]{2,1,0:T(8,128)(2,1)}), bf16[64,24,128]{2,1,0:T(8,128)(2,1)S(1)}, u32[]{:S(2)}, u32[]{:S(2)}) %all-to-all-start) | async-done | bytes 393248 | tf_op jit(solution)/shard_map/all_to_all | solution.py:228
  33.7 0.2 reshape.23
  33.8 0.2 convolution_convert_fusion
  34.1 5.2 %collective-permute-start = (bf16[96,1024]{1,0:T(8,128)(2,1)S(1)}, bf16[96,1024]{1,0:T(8,128)(2,1)S(1)}, u32[]{:S(2)}, u32[]{:S(2)}) collective-permute-start(bf16[96,1024]{1,0:T(8,128)(2,1)S(1)} %convolution_convert_fusion), channel_id=1, source_target_pairs={{0,64},{64,0},{128,192},{192,128},{256,320},{320,256},{384,448},{4... | collective-permute-start | bytes 589832 | tf_op jit(solution)/shard_map/ppermute | solution.py:218
  39.3 0.2 convolution_convert_fusion.1.mine
  39.5 0.8 collective-permute-done.partner
  40.4 4.4 %collective-permute-start.1 = (bf16[192,1024]{1,0:T(8,128)(2,1)S(1)}, bf16[192,1024]{1,0:T(8,128)(2,1)S(1)}, u32[]{:S(2)}, u32[]{:S(2)}) collective-permute-start(bf16[192,1024]{1,0:T(8,128)(2,1)S(1)} %pad_maximum_fusion), channel_id=1, source_target_pairs={{0,128},{64,448},{128,256},{192,64},{256,384},{320,192},{384,0},{4... | collective-permute-start | bytes 1179656 | tf_op jit(solution)/shard_map/ppermute | solution.py:218
  44.8 1.9 %collective-permute-start.2 = (bf16[96,1024]{1,0:T(8,128)(2,1)S(1)}, bf16[96,1024]{1,0:T(8,128)(2,1)S(1)}, u32[]{:S(2)}, u32[]{:S(2)}) collective-permute-start(bf16[96,1024]{1,0:T(8,128)(2,1)S(1)} %convolution_convert_fusion.1.mine), channel_id=1, source_target_pairs={{0,384},{64,192},{128,0},{192,320},{256,128},{320,448},{384,256},{... | collective-permute-start | bytes 589832 | tf_op jit(solution)/shard_map/ppermute | solution.py:218
  46.7 6.3 %collective-permute-done.2.far = bf16[96,1024]{1,0:T(8,128)(2,1)S(1)} collective-permute-done((bf16[96,1024]{1,0:T(8,128)(2,1)S(1)}, bf16[96,1024]{1,0:T(8,128)(2,1)S(1)}, u32[]{:S(2)}, u32[]{:S(2)}) %collective-permute-start.2) | collective-permute-done | bytes 196640 | tf_op jit(solution)/shard_map/ppermute | solution.py:218
  53.0 0.0 collective-permute-done.1.near
  53.0 1.4 %grams.1 = (bf16[1024,128]{1,0:T(8,128)(2,1)S(1)}, bf16[5,128,1024]{2,1,0:T(8,128)(2,1)S(1)}) custom-call(s32[1]{0:T(128)} %bitcast.core, bf16[96,1024]{1,0:T(8,128)(2,1)S(1)} %convolution_convert_fusion.1.mine, bf16[96,1024]{1,0:T(8,128)(2,1)S(1)} %collective-permute-done.partner, bf16[192,1024]{1,0:T(8,128)(2,1)S(1)} %collective-permute-done.1.near, ...), custom_call_target="tpu_custom_call" | custom-call | tf_op jit(solution)/shard_map/grams/pallas_call | solution.py:243
  54.4 18.5 %all_to_all.15 = bf16[64,16,128]{2,1,0:T(8,128)(2,1)S(1)} all-to-all(bf16[64,16,128]{2,1,0:T(8,128)(2,1)S(1)} %bitcast.16), channel_id=1, replica_groups=mesh['col'=8,'row'=64] {'row'}, dimensions={0} | all-to-all | bytes 524288 | tf_op jit(solution)/shard_map/all_to_all | solution.py:255
  72.9 0.1 convert_reduce_fusion
  73.1 21.1 %all_to_all.16 = f32[64,16,128]{2,1,0:T(8,128)S(1)} all-to-all(f32[64,16,128]{2,1,0:T(8,128)S(1)} %broadcast_in_dim.2), channel_id=1, replica_groups=mesh['col'=8,'row'=64] {'row'}, dimensions={0} | all-to-all | bytes 1048576 | tf_op jit(solution)/shard_map/all_to_all | solution.py:258
  94.2 8.9 %rounds.1 = (bf16[96,1024]{1,0:T(8,128)(2,1)S(1)}, bf16[96,1024]{1,0:T(8,128)(2,1)S(1)}) custom-call(s32[1]{0:T(128)} %bitcast.core, f32[1024,128]{1,0:T(8,128)S(1)} %bitcast.15, bf16[5,128,1024]{2,1,0:T(8,128)(2,1)S(1)} %get-tuple-element.10.rows_ref), custom_call_target="tpu_custom_call" | custom-call | tf_op jit(solution)/shard_map/rounds/pallas_call | solution.py:260
  103.1 5.4 %collective-permute-start.3 = (bf16[96,1024]{1,0:T(8,128)(2,1)S(1)}, bf16[96,1024]{1,0:T(8,128)(2,1)S(1)}, u32[]{:S(2)}, u32[]{:S(2)}) collective-permute-start(bf16[96,1024]{1,0:T(8,128)(2,1)S(1)} %get-tuple-element.12), channel_id=1, source_target_pairs={{0,64},{64,0},{128,192},{192,128},{256,320},{320,256},{384,448},{4... | collective-permute-start | bytes 589832 | tf_op jit(solution)/shard_map/ppermute | solution.py:218
  108.5 1.0 collective-permute-done.3
  109.6 0.8 pad_maximum_fusion.1
  (3 shorter events, 0.1 us)
Async XLA Ops:
  0.0 19.0 %copy-start = (s32[192]{0:T(256)S(1)}, s32[192]{0:T(256)}, u32[]{:S(2)}) copy-start(s32[192]{0:T(256)} %param.3) | copy-start | bytes 2308
  1.9 31.8 %all-to-all-start = ((bf16[64,24,128]{2,1,0:T(8,128)(2,1)}), bf16[64,24,128]{2,1,0:T(8,128)(2,1)S(1)}, u32[]{:S(2)}, u32[]{:S(2)}) async-start(bf16[64,24,128]{2,1,0:T(8,128)(2,1)} %copy_bitcast_fusion), calls=%async_computation | async-start | bytes 786432 | tf_op jit(solution)/shard_map/all_to_all | solution.py:228
  34.1 6.3 %collective-permute-start = (bf16[96,1024]{1,0:T(8,128)(2,1)S(1)}, bf16[96,1024]{1,0:T(8,128)(2,1)S(1)}, u32[]{:S(2)}, u32[]{:S(2)}) collective-permute-start(bf16[96,1024]{1,0:T(8,128)(2,1)S(1)} %convolution_convert_fusion), channel_id=1, source_target_pairs={{0,64},{64,0},{128,192},{192,128},{256,320},{320,256},{384,448},{4... | collective-permute-start | bytes 589832 | tf_op jit(solution)/shard_map/ppermute | solution.py:218
  40.4 12.7 %collective-permute-start.1 = (bf16[192,1024]{1,0:T(8,128)(2,1)S(1)}, bf16[192,1024]{1,0:T(8,128)(2,1)S(1)}, u32[]{:S(2)}, u32[]{:S(2)}) collective-permute-start(bf16[192,1024]{1,0:T(8,128)(2,1)S(1)} %pad_maximum_fusion), channel_id=1, source_target_pairs={{0,128},{64,448},{128,256},{192,64},{256,384},{320,192},{384,0},{4... | collective-permute-start | bytes 1179656 | tf_op jit(solution)/shard_map/ppermute | solution.py:218
  44.8 8.3 %collective-permute-start.2 = (bf16[96,1024]{1,0:T(8,128)(2,1)S(1)}, bf16[96,1024]{1,0:T(8,128)(2,1)S(1)}, u32[]{:S(2)}, u32[]{:S(2)}) collective-permute-start(bf16[96,1024]{1,0:T(8,128)(2,1)S(1)} %convolution_convert_fusion.1.mine), channel_id=1, source_target_pairs={{0,384},{64,192},{128,0},{192,320},{256,128},{320,448},{384,256},{... | collective-permute-start | bytes 589832 | tf_op jit(solution)/shard_map/ppermute | solution.py:218
  103.1 6.4 %collective-permute-start.3 = (bf16[96,1024]{1,0:T(8,128)(2,1)S(1)}, bf16[96,1024]{1,0:T(8,128)(2,1)S(1)}, u32[]{:S(2)}, u32[]{:S(2)}) collective-permute-start(bf16[96,1024]{1,0:T(8,128)(2,1)S(1)} %get-tuple-element.12), channel_id=1, source_target_pairs={{0,64},{64,0},{128,192},{192,128},{256,320},{320,256},{384,448},{4... | collective-permute-start | bytes 589832 | tf_op jit(solution)/shard_map/ppermute | solution.py:218

commit v7 on v6

--- a/solution.py
+++ b/solution.py
@@ -17,7 +17,6 @@
 SLOTS = 10
 CARRIERS, SPREAD, LAST = BLOCKS[:SLOTS], BLOCKS[SLOTS : SLOTS + 3], BLOCKS[SLOTS + 3]
 USED = SLOTS * PAIR + BLOCK
-EXTRA = 16
 
 
 def iota(shape, dim):
@@ -71,22 +70,14 @@
     for k in range(SLOTS):
         extra = shifted(block[SPREAD[k // 3]], PAIR - CHUNK * (k % 3)) if k < 9 else shifted(last, PAIR)
         whole = jnp.where(lane < PAIR, block[CARRIERS[k]], extra)
-        packed[k * PAIR : (k + 1) * PAIR, :] = whole.astype(packed.dtype)
+        packed[k * PAIR : (k + 1) * PAIR, :] = whole
     sides = jnp.where(
         lane[:BLOCK] < LANES // 2, shifted(last[:BLOCK], -CHUNK), shifted(last[BLOCK:], CHUNK)
     )
-    packed[SLOTS * PAIR : USED, :] = sides.astype(packed.dtype)
-    place = iota((EXTRA, LANES), 0)
-    on_diagonal = iota((PAIR, LANES), 0) == lane
-    lost = jnp.zeros((EXTRA, LANES), jnp.float32)
-    for s in range(SPAN):
-        value = block[s, s]
-        gone = jnp.where(on_diagonal, value - value.astype(packed.dtype).astype(jnp.float32), 0.0)
-        lost = jnp.where(place == s, jnp.sum(gone, axis=0, keepdims=True), lost)
-    packed[USED : USED + EXTRA, :] = lost.astype(packed.dtype)
-    tail = packed.shape[0] - USED - EXTRA
+    packed[SLOTS * PAIR : USED, :] = sides
+    tail = packed.shape[0] - USED
     if tail:
-        packed[USED + EXTRA :, :] = jnp.zeros((tail, LANES), packed.dtype)
+        packed[USED:, :] = jnp.zeros((tail, LANES), jnp.float32)
 
 
 def unpacked(packed):
@@ -106,9 +97,6 @@
     sides = jnp.concatenate([shifted(rest, CHUNK), shifted(rest, -CHUNK)], axis=0)
     value = jnp.where(lane < CHUNK, shifted(slot[SLOTS - 1], -PAIR), sides)
     gram[LAST] = jnp.where(lane < PAIR, value, 0.0)
-    on_diagonal = iota((PAIR, LANES), 0) == lane
-    for s in range(SPAN):
-        gram[s, s] += jnp.where(on_diagonal, packed[USED + s : USED + s + 1, :], 0.0)
     return {name: jnp.concatenate([value, floor], axis=0) for name, value in gram.items()}
 
 
@@ -236,14 +224,14 @@
     near = passed(jnp.concatenate([mine, partner], axis=0), lambda c: c + 2 if c % 2 == 0 else c - 2)
     held = (mine, partner, near, far)
     chosen = core.astype(jnp.int32).reshape(1)
-    share = -(-(USED + EXTRA) // (16 * row_count)) * 16
+    share = -(-USED // (8 * row_count)) * 8
     limit = pltpu.CompilerParams(vmem_limit_bytes=48 * 1024 * 1024)
     scalar = pl.BlockSpec(memory_space=pltpu.SMEM)
     vector = pl.BlockSpec(memory_space=pltpu.VMEM)
     packed, rows = pl.pallas_call(
         gram_kernel,
         out_shape=(
-            jax.ShapeDtypeStruct((share * row_count, LANES), jnp.bfloat16),
+            jax.ShapeDtypeStruct((share * row_count, LANES), jnp.float32),
             jax.ShapeDtypeStruct((SPAN, LANES, width), jnp.bfloat16),
         ),
         in_specs=[scalar] + [vector] * 4,
@@ -253,7 +241,7 @@
     )(chosen, *held)
     parts = packed.reshape(row_count, share, LANES)
     parts = lax.all_to_all(parts, "row", split_axis=0, concat_axis=0, tiled=True)
-    summed = jnp.sum(parts.astype(jnp.float32), axis=0)
+    summed = jnp.sum(parts, axis=0)
     copies = jnp.broadcast_to(summed[None], (row_count, share, LANES))
     whole = lax.all_to_all(copies, "row", split_axis=0, concat_axis=0, tiled=True)
     pair = jax.ShapeDtypeStruct((PAIR, width), jnp.bfloat16)

time: 111 us -> 116 us (1.045)
  blocking collectives: 39.7 us -> 45.1 us
    all_to_all x1, blocking collectives: 18.5 us -> 22.8 us  [on_device(): lax.all_to_all(parts, 'row', split_axis=0, concat_axis=0, tiled=True)]
    all_to_all x1, blocking collectives: 21.1 us -> 22.3 us  [on_device(): lax.all_to_all(copies, 'row', split_axis=0, concat_axis=0, tiled=True)]
where the time goes in v7:
time: 116 us
  blocking collectives  45.1 us (39%)
  starting transfers between devices  34.2 us (29%)
  waiting for transfers between devices  22.6 us (19%)
  Pallas kernels  10.3 us (9%)
  local copies, waits for them, and re-layouts  2.14 us (2%)
    all_to_all x1, blocking collectives, on_device(): lax.all_to_all(parts, 'row', split_axis=0, concat_axis=0, tiled=True)  22.8 us
    all_to_all x1, blocking collectives, on_device(): lax.all_to_all(copies, 'row', split_axis=0, concat_axis=0, tiled=True)  22.3 us
    all_to_all x1, starting transfers between devices, on_device(): lax.all_to_all(tiles, 'row', split_axis=0, concat_axis=0, tiled=True)  17.1 us
    ppermute x4, starting transfers between devices, passed(): lax.ppermute(value, 'col', [(source, where(source) % count) for source in...  17.1 us
    all_to_all x1, waiting for transfers between devices, on_device(): lax.all_to_all(tiles, 'row', split_axis=0, concat_axis=0, tiled=True)  14.4 us
    pallas_call x1, Pallas kernels, on_device(): pl.pallas_call(rounds_kernel, out_shape=(pair, pair), in_specs=[scalar, v...  8.92 us
    ppermute x4, waiting for transfers between devices, passed(): lax.ppermute(value, 'col', [(source, where(source) % count) for source in...  8.23 us
  transfers between devices with their start and end apart: 5, of which 4 were waited for; matrix products, arithmetic and copies ran while one was open for 0% of the time, Pallas kernels for 0%

profile of v7, /device:TPU:1, one launch (start us, length us, event | category | flops | bytes accessed | tf_op | source)
XLA Modules:
  0.0 116.0 jit_solution(1216902040273596822)
XLA Ops:
  0.0 0.0 copy-start
  0.0 1.9 %copy_bitcast_fusion = bf16[64,24,128]{2,1,0:T(8,128)(2,1)} fusion(bf16[1,3,512,128]{3,1,2,0:T(4,128)(2,1)} %bitcast.17), kind=kLoop, calls=%fused_computation.5 | loop fusion | bytes 786432 | tf_op jit(solution)/shard_map/reshape | solution.py:215
  1.9 17.1 %all-to-all-start = ((bf16[64,24,128]{2,1,0:T(8,128)(2,1)}), bf16[64,24,128]{2,1,0:T(8,128)(2,1)S(1)}, u32[]{:S(2)}, u32[]{:S(2)}) async-start(bf16[64,24,128]{2,1,0:T(8,128)(2,1)} %copy_bitcast_fusion), calls=%async_computation | async-start | bytes 786432 | tf_op jit(solution)/shard_map/all_to_all | solution.py:216
  19.0 0.0 copy-done
  19.0 0.1 fusion.2
  19.1 0.1 add_select_fusion
  19.2 0.1 iota_compare_fusion
  19.3 14.4 %all-to-all-done = bf16[64,24,128]{2,1,0:T(8,128)(2,1)S(1)} async-done(((bf16[64,24,128]{2,1,0:T(8,128)(2,1)}), bf16[64,24,128]{2,1,0:T(8,128)(2,1)S(1)}, u32[]{:S(2)}, u32[]{:S(2)}) %all-to-all-start) | async-done | bytes 393248 | tf_op jit(solution)/shard_map/all_to_all | solution.py:216
  33.7 0.2 reshape.23
  33.8 0.2 convolution_convert_fusion
  34.1 5.2 %collective-permute-start = (bf16[96,1024]{1,0:T(8,128)(2,1)S(1)}, bf16[96,1024]{1,0:T(8,128)(2,1)S(1)}, u32[]{:S(2)}, u32[]{:S(2)}) collective-permute-start(bf16[96,1024]{1,0:T(8,128)(2,1)S(1)} %convolution_convert_fusion), channel_id=1, source_target_pairs={{0,64},{64,0},{128,192},{192,128},{256,320},{320,256},{384,448},{4... | collective-permute-start | bytes 589832 | tf_op jit(solution)/shard_map/ppermute | solution.py:206
  39.3 0.2 convolution_convert_fusion.1.mine
  39.5 0.8 collective-permute-done.partner
  40.4 4.4 %collective-permute-start.1 = (bf16[192,1024]{1,0:T(8,128)(2,1)S(1)}, bf16[192,1024]{1,0:T(8,128)(2,1)S(1)}, u32[]{:S(2)}, u32[]{:S(2)}) collective-permute-start(bf16[192,1024]{1,0:T(8,128)(2,1)S(1)} %pad_maximum_fusion), channel_id=1, source_target_pairs={{0,128},{64,448},{128,256},{192,64},{256,384},{320,192},{384,0},{4... | collective-permute-start | bytes 1179656 | tf_op jit(solution)/shard_map/ppermute | solution.py:206
  44.8 1.9 %collective-permute-start.2 = (bf16[96,1024]{1,0:T(8,128)(2,1)S(1)}, bf16[96,1024]{1,0:T(8,128)(2,1)S(1)}, u32[]{:S(2)}, u32[]{:S(2)}) collective-permute-start(bf16[96,1024]{1,0:T(8,128)(2,1)S(1)} %convolution_convert_fusion.1.mine), channel_id=1, source_target_pairs={{0,384},{64,192},{128,0},{192,320},{256,128},{320,448},{384,256},{... | collective-permute-start | bytes 589832 | tf_op jit(solution)/shard_map/ppermute | solution.py:206
  46.7 6.3 %collective-permute-done.2.far = bf16[96,1024]{1,0:T(8,128)(2,1)S(1)} collective-permute-done((bf16[96,1024]{1,0:T(8,128)(2,1)S(1)}, bf16[96,1024]{1,0:T(8,128)(2,1)S(1)}, u32[]{:S(2)}, u32[]{:S(2)}) %collective-permute-start.2) | collective-permute-done | bytes 196640 | tf_op jit(solution)/shard_map/ppermute | solution.py:206
  53.0 0.0 collective-permute-done.1.near
  53.0 1.4 %grams.1 = (f32[1024,128]{1,0:T(8,128)S(1)}, bf16[5,128,1024]{2,1,0:T(8,128)(2,1)S(1)}) custom-call(s32[1]{0:T(128)} %bitcast.core, bf16[96,1024]{1,0:T(8,128)(2,1)S(1)} %convolution_convert_fusion.1.mine, bf16[96,1024]{1,0:T(8,128)(2,1)S(1)} %collective-permute-done.partner, bf16[192,1024]{1,0:T(8,128)(2,1)S(1)} %collective-permute-done.1.near, ...), custom_call_target="tpu_custom_call" | custom-call | tf_op jit(solution)/shard_map/grams/pallas_call | solution.py:231
  54.4 22.8 %all_to_all.15 = f32[64,16,128]{2,1,0:T(8,128)S(1)} all-to-all(f32[64,16,128]{2,1,0:T(8,128)S(1)} %bitcast.16), channel_id=1, replica_groups=mesh['col'=8,'row'=64] {'row'}, dimensions={0} | all-to-all | bytes 1048576 | tf_op jit(solution)/shard_map/all_to_all | solution.py:243
  77.2 0.1 reduce_sum.9
  77.3 22.3 %all_to_all.16 = f32[64,16,128]{2,1,0:T(8,128)S(1)} all-to-all(f32[64,16,128]{2,1,0:T(8,128)S(1)} %broadcast_in_dim.2), channel_id=1, replica_groups=mesh['col'=8,'row'=64] {'row'}, dimensions={0} | all-to-all | bytes 1048576 | tf_op jit(solution)/shard_map/all_to_all | solution.py:246
  99.7 8.9 %rounds.1 = (bf16[96,1024]{1,0:T(8,128)(2,1)S(1)}, bf16[96,1024]{1,0:T(8,128)(2,1)S(1)}) custom-call(s32[1]{0:T(128)} %bitcast.core, f32[1024,128]{1,0:T(8,128)S(1)} %bitcast.15, bf16[5,128,1024]{2,1,0:T(8,128)(2,1)S(1)} %get-tuple-element.10.rows_ref), custom_call_target="tpu_custom_call" | custom-call | tf_op jit(solution)/shard_map/rounds/pallas_call | solution.py:248
  108.6 5.5 %collective-permute-start.3 = (bf16[96,1024]{1,0:T(8,128)(2,1)S(1)}, bf16[96,1024]{1,0:T(8,128)(2,1)S(1)}, u32[]{:S(2)}, u32[]{:S(2)}) collective-permute-start(bf16[96,1024]{1,0:T(8,128)(2,1)S(1)} %get-tuple-element.12), channel_id=1, source_target_pairs={{0,64},{64,0},{128,192},{192,128},{256,320},{320,256},{384,448},{4... | collective-permute-start | bytes 589832 | tf_op jit(solution)/shard_map/ppermute | solution.py:206
  114.1 1.0 collective-permute-done.3
  115.2 0.8 pad_maximum_fusion.1
  (3 shorter events, 0.1 us)
Async XLA Ops:
  0.0 19.0 %copy-start = (s32[192]{0:T(256)S(1)}, s32[192]{0:T(256)}, u32[]{:S(2)}) copy-start(s32[192]{0:T(256)} %param.3) | copy-start | bytes 2308
  1.9 31.8 %all-to-all-start = ((bf16[64,24,128]{2,1,0:T(8,128)(2,1)}), bf16[64,24,128]{2,1,0:T(8,128)(2,1)S(1)}, u32[]{:S(2)}, u32[]{:S(2)}) async-start(bf16[64,24,128]{2,1,0:T(8,128)(2,1)} %copy_bitcast_fusion), calls=%async_computation | async-start | bytes 786432 | tf_op jit(solution)/shard_map/all_to_all | solution.py:216
  34.1 6.3 %collective-permute-start = (bf16[96,1024]{1,0:T(8,128)(2,1)S(1)}, bf16[96,1024]{1,0:T(8,128)(2,1)S(1)}, u32[]{:S(2)}, u32[]{:S(2)}) collective-permute-start(bf16[96,1024]{1,0:T(8,128)(2,1)S(1)} %convolution_convert_fusion), channel_id=1, source_target_pairs={{0,64},{64,0},{128,192},{192,128},{256,320},{320,256},{384,448},{4... | collective-permute-start | bytes 589832 | tf_op jit(solution)/shard_map/ppermute | solution.py:206
  40.4 12.7 %collective-permute-start.1 = (bf16[192,1024]{1,0:T(8,128)(2,1)S(1)}, bf16[192,1024]{1,0:T(8,128)(2,1)S(1)}, u32[]{:S(2)}, u32[]{:S(2)}) collective-permute-start(bf16[192,1024]{1,0:T(8,128)(2,1)S(1)} %pad_maximum_fusion), channel_id=1, source_target_pairs={{0,128},{64,448},{128,256},{192,64},{256,384},{320,192},{384,0},{4... | collective-permute-start | bytes 1179656 | tf_op jit(solution)/shard_map/ppermute | solution.py:206
  44.8 8.3 %collective-permute-start.2 = (bf16[96,1024]{1,0:T(8,128)(2,1)S(1)}, bf16[96,1024]{1,0:T(8,128)(2,1)S(1)}, u32[]{:S(2)}, u32[]{:S(2)}) collective-permute-start(bf16[96,1024]{1,0:T(8,128)(2,1)S(1)} %convolution_convert_fusion.1.mine), channel_id=1, source_target_pairs={{0,384},{64,192},{128,0},{192,320},{256,128},{320,448},{384,256},{... | collective-permute-start | bytes 589832 | tf_op jit(solution)/shard_map/ppermute | solution.py:206
  108.6 6.6 %collective-permute-start.3 = (bf16[96,1024]{1,0:T(8,128)(2,1)S(1)}, bf16[96,1024]{1,0:T(8,128)(2,1)S(1)}, u32[]{:S(2)}, u32[]{:S(2)}) collective-permute-start(bf16[96,1024]{1,0:T(8,128)(2,1)S(1)} %get-tuple-element.12), channel_id=1, source_target_pairs={{0,64},{64,0},{128,192},{192,128},{256,320},{320,256},{384,448},{4... | collective-permute-start | bytes 589832 | tf_op jit(solution)/shard_map/ppermute | solution.py:206

commit v8 on v7

--- a/solution.py
+++ b/solution.py
@@ -12,11 +12,12 @@
 SPAN = 5
 CHUNK = LANES - PAIR
 
-BLOCKS = [(s, t) for s in range(SPAN) for t in range(s + 1, min(s + ROUNDS, SPAN))]
-BLOCKS += [(s, s) for s in range(SPAN)]
-SLOTS = 10
-CARRIERS, SPREAD, LAST = BLOCKS[:SLOTS], BLOCKS[SLOTS : SLOTS + 3], BLOCKS[SLOTS + 3]
-USED = SLOTS * PAIR + BLOCK
+CROSS = [(s, t) for s in range(SPAN) for t in range(s + 1, min(s + ROUNDS, SPAN))]
+LEFT, RIGHT = CROSS[:7], [(s, s) for s in range(SPAN)] + CROSS[7:]
+HALF = LANES // 2
+STEP = PAIR + BLOCK
+USED = len(LEFT) * STEP
+GROUP = 16
 
 
 def iota(shape, dim):
@@ -66,37 +67,46 @@
         for t in range(s, end):
             block[s, t] = strip[:, (t - s) * LANES : (t - s + 1) * LANES]
     lane = iota((PAIR, LANES), 1)
-    last = block[LAST]
-    for k in range(SLOTS):
-        extra = shifted(block[SPREAD[k // 3]], PAIR - CHUNK * (k % 3)) if k < 9 else shifted(last, PAIR)
-        whole = jnp.where(lane < PAIR, block[CARRIERS[k]], extra)
-        packed[k * PAIR : (k + 1) * PAIR, :] = whole
-    sides = jnp.where(
-        lane[:BLOCK] < LANES // 2, shifted(last[:BLOCK], -CHUNK), shifted(last[BLOCK:], CHUNK)
-    )
-    packed[SLOTS * PAIR : USED, :] = sides
-    tail = packed.shape[0] - USED
-    if tail:
-        packed[USED:, :] = jnp.zeros((tail, LANES), jnp.float32)
+    short = lane[:BLOCK]
+    flat = []
+    for one, two in zip(LEFT, RIGHT):
+        one, two = block[one], block[two]
+        flat.append(jnp.where(lane < HALF, one, shifted(two, HALF)))
+        first = jnp.where(short < CHUNK, shifted(one[:BLOCK], -HALF), shifted(one[BLOCK:], -CHUNK))
+        second = jnp.where(short < PAIR, two[:BLOCK], shifted(two[BLOCK:], CHUNK))
+        flat.append(jnp.where(short < HALF, first, second))
+    groups = packed.shape[0] // (3 * GROUP // 2)
+    flat.append(jnp.zeros((groups * GROUP - USED, LANES), jnp.float32))
+    flat = jnp.concatenate(flat, axis=0)
+    left = iota((GROUP // 2, LANES), 1) < HALF
+    for pair in range(groups // 2):
+        rows = []
+        for at in (2 * pair * GROUP, (2 * pair + 1) * GROUP):
+            value = flat[at : at + GROUP]
+            lost = value - value.astype(jnp.bfloat16).astype(jnp.float32)
+            lost = jnp.where(left, shifted(lost[: GROUP // 2], HALF), lost[GROUP // 2 :])
+            rows += [value, lost]
+        packed[3 * GROUP * pair : 3 * GROUP * (pair + 1), :] = jnp.concatenate(rows, axis=0).astype(jnp.bfloat16)
+
+
+def restored(sums):
+    sums = sums.reshape(-1, 3 * GROUP // 2, LANES)
+    high, lost = sums[:, :GROUP], sums[:, GROUP:]
+    lost = jnp.concatenate([lost[:, :, :HALF], lost[:, :, HALF:]], axis=1)
+    return (high + jnp.pad(lost, ((0, 0), (0, 0), (HALF, 0)))).reshape(-1, LANES)
 
 
 def unpacked(packed):
     lane = iota((PAIR, LANES), 1)
     floor = jnp.zeros((CHUNK, LANES), jnp.float32)
-    slot = [packed[k * PAIR : (k + 1) * PAIR, :] for k in range(SLOTS)]
     gram = {}
-    for k, name in enumerate(CARRIERS):
-        gram[name] = jnp.where(lane < PAIR, slot[k], 0.0)
-    for m, name in enumerate(SPREAD):
-        value = jnp.zeros((PAIR, LANES), jnp.float32)
-        for j in range(3):
-            here = (lane >= CHUNK * j) & (lane < CHUNK * (j + 1))
-            value = jnp.where(here, shifted(slot[3 * m + j], CHUNK * j - PAIR), value)
-        gram[name] = value
-    rest = packed[SLOTS * PAIR : USED, :]
-    sides = jnp.concatenate([shifted(rest, CHUNK), shifted(rest, -CHUNK)], axis=0)
-    value = jnp.where(lane < CHUNK, shifted(slot[SLOTS - 1], -PAIR), sides)
-    gram[LAST] = jnp.where(lane < PAIR, value, 0.0)
+    for k, (one, two) in enumerate(zip(LEFT, RIGHT)):
+        main = packed[k * STEP : k * STEP + PAIR, :]
+        rest = packed[k * STEP + PAIR : (k + 1) * STEP, :]
+        sides = jnp.concatenate([shifted(rest, HALF), shifted(rest, CHUNK)], axis=0)
+        gram[one] = jnp.where(lane < HALF, main, jnp.where(lane < PAIR, sides, 0.0))
+        sides = jnp.concatenate([rest, shifted(rest, -CHUNK)], axis=0)
+        gram[two] = jnp.where(lane < HALF, shifted(main, HALF), jnp.where(lane < PAIR, sides, 0.0))
     return {name: jnp.concatenate([value, floor], axis=0) for name, value in gram.items()}
 
 
@@ -224,14 +234,14 @@
     near = passed(jnp.concatenate([mine, partner], axis=0), lambda c: c + 2 if c % 2 == 0 else c - 2)
     held = (mine, partner, near, far)
     chosen = core.astype(jnp.int32).reshape(1)
-    share = -(-USED // (8 * row_count)) * 8
+    share = -(-USED // (GROUP * row_count)) * GROUP
     limit = pltpu.CompilerParams(vmem_limit_bytes=48 * 1024 * 1024)
     scalar = pl.BlockSpec(memory_space=pltpu.SMEM)
     vector = pl.BlockSpec(memory_space=pltpu.VMEM)
     packed, rows = pl.pallas_call(
         gram_kernel,
         out_shape=(
-            jax.ShapeDtypeStruct((share * row_count, LANES), jnp.float32),
+            jax.ShapeDtypeStruct((share * 3 // 2 * row_count, LANES), jnp.bfloat16),
             jax.ShapeDtypeStruct((SPAN, LANES, width), jnp.bfloat16),
         ),
         in_specs=[scalar] + [vector] * 4,
@@ -239,9 +249,9 @@
         compiler_params=limit,
         name="grams",
     )(chosen, *held)
-    parts = packed.reshape(row_count, share, LANES)
+    parts = packed.reshape(row_count, share * 3 // 2, LANES)
     parts = lax.all_to_all(parts, "row", split_axis=0, concat_axis=0, tiled=True)
-    summed = jnp.sum(parts, axis=0)
+    summed = restored(jnp.sum(parts.astype(jnp.float32), axis=0))
     copies = jnp.broadcast_to(summed[None], (row_count, share, LANES))
     whole = lax.all_to_all(copies, "row", split_axis=0, concat_axis=0, tiled=True)
     pair = jax.ShapeDtypeStruct((PAIR, width), jnp.bfloat16)

time: 116 us -> 114 us (0.983)
  blocking collectives: 45.1 us -> 42.4 us
    all_to_all x1, blocking collectives: 22.8 us -> 20.5 us  [on_device(): lax.all_to_all(parts, 'row', split_axis=0, concat_axis=0, tiled=True)]
where the time goes in v8:
time: 114 us; the launch traced here: 113 us
  blocking collectives  42.4 us (37%)
  starting transfers between devices  34.1 us (30%)
  waiting for transfers between devices  22.6 us (20%)
  Pallas kernels  10.3 us (9%)
  local copies, waits for them, and re-layouts  2.22 us (2%)
  other arithmetic  1.17 us (1%)
    all_to_all x1, blocking collectives, on_device(): lax.all_to_all(copies, 'row', split_axis=0, concat_axis=0, tiled=True)  22 us
    all_to_all x1, blocking collectives, on_device(): lax.all_to_all(parts, 'row', split_axis=0, concat_axis=0, tiled=True)  20.5 us
    all_to_all x1, starting transfers between devices, on_device(): lax.all_to_all(tiles, 'row', split_axis=0, concat_axis=0, tiled=True)  17.1 us
    ppermute x4, starting transfers between devices, passed(): lax.ppermute(value, 'col', [(source, where(source) % count) for source in...  17 us
    all_to_all x1, waiting for transfers between devices, on_device(): lax.all_to_all(tiles, 'row', split_axis=0, concat_axis=0, tiled=True)  14.4 us
    pallas_call x1, Pallas kernels, on_device(): pl.pallas_call(rounds_kernel, out_shape=(pair, pair), in_specs=[scalar, v...  8.88 us
    ppermute x4, waiting for transfers between devices, passed(): lax.ppermute(value, 'col', [(source, where(source) % count) for source in...  8.23 us
  transfers between devices with their start and end apart: 5, of which 4 were waited for; matrix products, arithmetic and copies ran while one was open for 0% of the time, Pallas kernels for 0%

profile of v8, /device:TPU:1, one launch (start us, length us, event | category | flops | bytes accessed | tf_op | source)
XLA Modules:
  0.0 113.4 jit_solution(12337705481835439926)
XLA Ops:
  0.0 0.0 copy-start
  0.0 1.9 %copy_bitcast_fusion = bf16[64,24,128]{2,1,0:T(8,128)(2,1)} fusion(bf16[1,3,512,128]{3,1,2,0:T(4,128)(2,1)} %bitcast.20), kind=kLoop, calls=%fused_computation.6 | loop fusion | bytes 786432 | tf_op jit(solution)/shard_map/reshape | solution.py:225
  1.9 17.1 %all-to-all-start = ((bf16[64,24,128]{2,1,0:T(8,128)(2,1)}), bf16[64,24,128]{2,1,0:T(8,128)(2,1)S(1)}, u32[]{:S(2)}, u32[]{:S(2)}) async-start(bf16[64,24,128]{2,1,0:T(8,128)(2,1)} %copy_bitcast_fusion), calls=%async_computation | async-start | bytes 786432 | tf_op jit(solution)/shard_map/all_to_all | solution.py:226
  19.0 0.0 copy-done
  19.0 0.1 fusion.5
  19.1 0.1 add_select_fusion
  19.2 0.1 iota_compare_fusion
  19.3 14.4 %all-to-all-done = bf16[64,24,128]{2,1,0:T(8,128)(2,1)S(1)} async-done(((bf16[64,24,128]{2,1,0:T(8,128)(2,1)}), bf16[64,24,128]{2,1,0:T(8,128)(2,1)S(1)}, u32[]{:S(2)}, u32[]{:S(2)}) %all-to-all-start) | async-done | bytes 393248 | tf_op jit(solution)/shard_map/all_to_all | solution.py:226
  33.7 0.2 reshape.25
  33.8 0.2 convolution_convert_fusion
  34.1 5.2 %collective-permute-start = (bf16[96,1024]{1,0:T(8,128)(2,1)S(1)}, bf16[96,1024]{1,0:T(8,128)(2,1)S(1)}, u32[]{:S(2)}, u32[]{:S(2)}) collective-permute-start(bf16[96,1024]{1,0:T(8,128)(2,1)S(1)} %convolution_convert_fusion), channel_id=1, source_target_pairs={{0,64},{64,0},{128,192},{192,128},{256,320},{320,256},{384,448},{4... | collective-permute-start | bytes 589832 | tf_op jit(solution)/shard_map/ppermute | solution.py:216
  39.3 0.2 convolution_convert_fusion.1.mine
  39.5 0.8 collective-permute-done.partner
  40.4 4.4 %collective-permute-start.1 = (bf16[192,1024]{1,0:T(8,128)(2,1)S(1)}, bf16[192,1024]{1,0:T(8,128)(2,1)S(1)}, u32[]{:S(2)}, u32[]{:S(2)}) collective-permute-start(bf16[192,1024]{1,0:T(8,128)(2,1)S(1)} %pad_maximum_fusion), channel_id=1, source_target_pairs={{0,128},{64,448},{128,256},{192,64},{256,384},{320,192},{384,0},{4... | collective-permute-start | bytes 1179656 | tf_op jit(solution)/shard_map/ppermute | solution.py:216
  44.8 1.9 %collective-permute-start.2 = (bf16[96,1024]{1,0:T(8,128)(2,1)S(1)}, bf16[96,1024]{1,0:T(8,128)(2,1)S(1)}, u32[]{:S(2)}, u32[]{:S(2)}) collective-permute-start(bf16[96,1024]{1,0:T(8,128)(2,1)S(1)} %convolution_convert_fusion.1.mine), channel_id=1, source_target_pairs={{0,384},{64,192},{128,0},{192,320},{256,128},{320,448},{384,256},{... | collective-permute-start | bytes 589832 | tf_op jit(solution)/shard_map/ppermute | solution.py:216
  46.7 6.3 %collective-permute-done.2.far = bf16[96,1024]{1,0:T(8,128)(2,1)S(1)} collective-permute-done((bf16[96,1024]{1,0:T(8,128)(2,1)S(1)}, bf16[96,1024]{1,0:T(8,128)(2,1)S(1)}, u32[]{:S(2)}, u32[]{:S(2)}) %collective-permute-start.2) | collective-permute-done | bytes 196640 | tf_op jit(solution)/shard_map/ppermute | solution.py:216
  53.0 0.0 collective-permute-done.1.near
  53.0 1.4 %grams.1 = (bf16[1536,128]{1,0:T(8,128)(2,1)S(1)}, bf16[5,128,1024]{2,1,0:T(8,128)(2,1)S(1)}) custom-call(s32[1]{0:T(128)} %bitcast.core, bf16[96,1024]{1,0:T(8,128)(2,1)S(1)} %convolution_convert_fusion.1.mine, bf16[96,1024]{1,0:T(8,128)(2,1)S(1)} %collective-permute-done.partner, bf16[192,1024]{1,0:T(8,128)(2,1)S(1)} %collective-permute-done.1.near, ...), custom_call_target="tpu_custom_call" | custom-call | tf_op jit(solution)/shard_map/grams/pallas_call | solution.py:241
  54.5 20.5 %all_to_all.15 = bf16[64,24,128]{2,1,0:T(8,128)(2,1)S(1)} all-to-all(bf16[64,24,128]{2,1,0:T(8,128)(2,1)S(1)} %bitcast.19), channel_id=1, replica_groups=mesh['col'=8,'row'=64] {'row'}, dimensions={0} | all-to-all | bytes 786432 | tf_op jit(solution)/shard_map/all_to_all | solution.py:253
  75.0 0.1 convert_reduce_fusion
  75.1 0.1 fusion.4
  75.1 0.1 fusion.3
  75.3 22.0 %all_to_all.16 = f32[64,16,128]{2,1,0:T(8,128)S(1)} all-to-all(f32[64,16,128]{2,1,0:T(8,128)S(1)} %broadcast_in_dim.9), channel_id=1, replica_groups=mesh['col'=8,'row'=64] {'row'}, dimensions={0} | all-to-all | bytes 1048576 | tf_op jit(solution)/shard_map/all_to_all | solution.py:256
  97.2 8.9 %rounds.1 = (bf16[96,1024]{1,0:T(8,128)(2,1)S(1)}, bf16[96,1024]{1,0:T(8,128)(2,1)S(1)}) custom-call(s32[1]{0:T(128)} %bitcast.core, f32[1024,128]{1,0:T(8,128)S(1)} %bitcast.18, bf16[5,128,1024]{2,1,0:T(8,128)(2,1)S(1)} %get-tuple-element.10.rows_ref), custom_call_target="tpu_custom_call" | custom-call | tf_op jit(solution)/shard_map/rounds/pallas_call | solution.py:258
  106.1 5.4 %collective-permute-start.3 = (bf16[96,1024]{1,0:T(8,128)(2,1)S(1)}, bf16[96,1024]{1,0:T(8,128)(2,1)S(1)}, u32[]{:S(2)}, u32[]{:S(2)}) collective-permute-start(bf16[96,1024]{1,0:T(8,128)(2,1)S(1)} %get-tuple-element.12), channel_id=1, source_target_pairs={{0,64},{64,0},{128,192},{192,128},{256,320},{320,256},{384,448},{4... | collective-permute-start | bytes 589832 | tf_op jit(solution)/shard_map/ppermute | solution.py:216
  111.5 1.0 collective-permute-done.3
  112.6 0.8 pad_maximum_fusion.1
  (3 shorter events, 0.1 us)
Async XLA Ops:
  0.0 19.0 %copy-start = (s32[192]{0:T(256)S(1)}, s32[192]{0:T(256)}, u32[]{:S(2)}) copy-start(s32[192]{0:T(256)} %param.3) | copy-start | bytes 2308
  1.9 31.8 %all-to-all-start = ((bf16[64,24,128]{2,1,0:T(8,128)(2,1)}), bf16[64,24,128]{2,1,0:T(8,128)(2,1)S(1)}, u32[]{:S(2)}, u32[]{:S(2)}) async-start(bf16[64,24,128]{2,1,0:T(8,128)(2,1)} %copy_bitcast_fusion), calls=%async_computation | async-start | bytes 786432 | tf_op jit(solution)/shard_map/all_to_all | solution.py:226
  34.1 6.3 %collective-permute-start = (bf16[96,1024]{1,0:T(8,128)(2,1)S(1)}, bf16[96,1024]{1,0:T(8,128)(2,1)S(1)}, u32[]{:S(2)}, u32[]{:S(2)}) collective-permute-start(bf16[96,1024]{1,0:T(8,128)(2,1)S(1)} %convolution_convert_fusion), channel_id=1, source_target_pairs={{0,64},{64,0},{128,192},{192,128},{256,320},{320,256},{384,448},{4... | collective-permute-start | bytes 589832 | tf_op jit(solution)/shard_map/ppermute | solution.py:216
  40.4 12.7 %collective-permute-start.1 = (bf16[192,1024]{1,0:T(8,128)(2,1)S(1)}, bf16[192,1024]{1,0:T(8,128)(2,1)S(1)}, u32[]{:S(2)}, u32[]{:S(2)}) collective-permute-start(bf16[192,1024]{1,0:T(8,128)(2,1)S(1)} %pad_maximum_fusion), channel_id=1, source_target_pairs={{0,128},{64,448},{128,256},{192,64},{256,384},{320,192},{384,0},{4... | collective-permute-start | bytes 1179656 | tf_op jit(solution)/shard_map/ppermute | solution.py:216
  44.8 8.3 %collective-permute-start.2 = (bf16[96,1024]{1,0:T(8,128)(2,1)S(1)}, bf16[96,1024]{1,0:T(8,128)(2,1)S(1)}, u32[]{:S(2)}, u32[]{:S(2)}) collective-permute-start(bf16[96,1024]{1,0:T(8,128)(2,1)S(1)} %convolution_convert_fusion.1.mine), channel_id=1, source_target_pairs={{0,384},{64,192},{128,0},{192,320},{256,128},{320,448},{384,256},{... | collective-permute-start | bytes 589832 | tf_op jit(solution)/shard_map/ppermute | solution.py:216
  106.1 6.5 %collective-permute-start.3 = (bf16[96,1024]{1,0:T(8,128)(2,1)S(1)}, bf16[96,1024]{1,0:T(8,128)(2,1)S(1)}, u32[]{:S(2)}, u32[]{:S(2)}) collective-permute-start(bf16[96,1024]{1,0:T(8,128)(2,1)S(1)} %get-tuple-element.12), channel_id=1, source_target_pairs={{0,64},{64,0},{128,192},{192,128},{256,320},{320,256},{384,448},{4... | collective-permute-start | bytes 589832 | tf_op jit(solution)/shard_map/ppermute | solution.py:216

commit v9 on v8

--- a/solution.py
+++ b/solution.py
@@ -152,30 +152,26 @@
 
 def next_grams(gram, turned, count, reach):
     top_lane = iota((LANES, LANES), 1) < BLOCK
-    top_half = iota((BLOCK, LANES), 1) < BLOCK
     floor = jnp.zeros((CHUNK, LANES), jnp.float32)
     right = {}
     for t in range(count):
         low = max(0, t - reach)
+        blocks = [gram[s, t] for s in range(low, t + 1)]
+        if t + 1 < count:
+            blocks.append(gram[t, t + 1].T)
         stack = []
-        for s in range(low, t + 1):
-            stack += halves(gram[s, t])
+        for block in blocks:
+            stack += halves(block)
         both = mm_nt(jnp.concatenate(stack, axis=0), turned[t])
-        for s in range(low, t + 1):
-            at = 2 * (s - low) * LANES
-            right[s, t] = both[at : at + LANES] + both[at + LANES : at + 2 * LANES]
+        for at in range(len(blocks)):
+            high = both[2 * at * LANES : (2 * at + 1) * LANES]
+            right[low + at, t] = high + both[(2 * at + 1) * LANES : (2 * at + 2) * LANES]
     following = {}
     for i in range(count - 1):
         upper, lower = turned[i][0:BLOCK], turned[i + 1][BLOCK:PAIR]
         for j in range(i, min(i + reach, count - 1)):
             top = turned_from_left(upper, jnp.where(top_lane, right[i, j], right[i, j + 1]))
-            if i == j:
-                bottom = turned_from_left(lower, right[i + 1, j + 1])
-                empty = jnp.zeros((LANES - BLOCK, LANES), jnp.float32)
-                mirrored = jnp.concatenate([top, empty], axis=0).T[BLOCK:PAIR]
-                bottom = jnp.where(top_half, mirrored, bottom)
-            else:
-                bottom = turned_from_left(lower, jnp.where(top_lane, right[i + 1, j], right[i + 1, j + 1]))
+            bottom = turned_from_left(lower, jnp.where(top_lane, right[i + 1, j], right[i + 1, j + 1]))
             following[i, j] = jnp.concatenate([top, bottom, floor], axis=0)
     return following
 

time: 114 us -> 114 us (level)
  no operation moved by 1% of the time
where the time goes in v9:
time: 114 us; the launch traced here: 113 us
  blocking collectives  42.4 us (37%)
  starting transfers between devices  34.1 us (30%)
  waiting for transfers between devices  22.6 us (20%)
  Pallas kernels  10.3 us (9%)
  local copies, waits for them, and re-layouts  2.22 us (2%)
  other arithmetic  1.17 us (1%)
    all_to_all x1, blocking collectives, on_device(): lax.all_to_all(copies, 'row', split_axis=0, concat_axis=0, tiled=True)  22 us
    all_to_all x1, blocking collectives, on_device(): lax.all_to_all(parts, 'row', split_axis=0, concat_axis=0, tiled=True)  20.5 us
    all_to_all x1, starting transfers between devices, on_device(): lax.all_to_all(tiles, 'row', split_axis=0, concat_axis=0, tiled=True)  17.1 us
    ppermute x4, starting transfers between devices, passed(): lax.ppermute(value, 'col', [(source, where(source) % count) for source in...  16.9 us
    all_to_all x1, waiting for transfers between devices, on_device(): lax.all_to_all(tiles, 'row', split_axis=0, concat_axis=0, tiled=True)  14.4 us
    pallas_call x1, Pallas kernels, on_device(): pl.pallas_call(rounds_kernel, out_shape=(pair, pair), in_specs=[scalar, v...  8.84 us
    ppermute x4, waiting for transfers between devices, passed(): lax.ppermute(value, 'col', [(source, where(source) % count) for source in...  8.23 us
  transfers between devices with their start and end apart: 5, of which 4 were waited for; matrix products, arithmetic and copies ran while one was open for 0% of the time, Pallas kernels for 0%

profile of v9, /device:TPU:1, one launch (start us, length us, event | category | flops | bytes accessed | tf_op | source)
XLA Modules:
  0.0 113.3 jit_solution(16902410108256418103)
XLA Ops:
  0.0 0.0 copy-start
  0.0 1.9 %copy_bitcast_fusion = bf16[64,24,128]{2,1,0:T(8,128)(2,1)} fusion(bf16[1,3,512,128]{3,1,2,0:T(4,128)(2,1)} %bitcast.20), kind=kLoop, calls=%fused_computation.6 | loop fusion | bytes 786432 | tf_op jit(solution)/shard_map/reshape | solution.py:221
  1.9 17.1 %all-to-all-start = ((bf16[64,24,128]{2,1,0:T(8,128)(2,1)}), bf16[64,24,128]{2,1,0:T(8,128)(2,1)S(1)}, u32[]{:S(2)}, u32[]{:S(2)}) async-start(bf16[64,24,128]{2,1,0:T(8,128)(2,1)} %copy_bitcast_fusion), calls=%async_computation | async-start | bytes 786432 | tf_op jit(solution)/shard_map/all_to_all | solution.py:222
  19.0 0.0 copy-done
  19.0 0.1 fusion.5
  19.1 0.1 add_select_fusion
  19.2 0.1 iota_compare_fusion
  19.3 14.4 %all-to-all-done = bf16[64,24,128]{2,1,0:T(8,128)(2,1)S(1)} async-done(((bf16[64,24,128]{2,1,0:T(8,128)(2,1)}), bf16[64,24,128]{2,1,0:T(8,128)(2,1)S(1)}, u32[]{:S(2)}, u32[]{:S(2)}) %all-to-all-start) | async-done | bytes 393248 | tf_op jit(solution)/shard_map/all_to_all | solution.py:222
  33.7 0.2 reshape.25
  33.8 0.2 convolution_convert_fusion
  34.1 5.2 %collective-permute-start = (bf16[96,1024]{1,0:T(8,128)(2,1)S(1)}, bf16[96,1024]{1,0:T(8,128)(2,1)S(1)}, u32[]{:S(2)}, u32[]{:S(2)}) collective-permute-start(bf16[96,1024]{1,0:T(8,128)(2,1)S(1)} %convolution_convert_fusion), channel_id=1, source_target_pairs={{0,64},{64,0},{128,192},{192,128},{256,320},{320,256},{384,448},{4... | collective-permute-start | bytes 589832 | tf_op jit(solution)/shard_map/ppermute | solution.py:212
  39.3 0.2 convolution_convert_fusion.1.mine
  39.5 0.8 collective-permute-done.partner
  40.4 4.4 %collective-permute-start.1 = (bf16[192,1024]{1,0:T(8,128)(2,1)S(1)}, bf16[192,1024]{1,0:T(8,128)(2,1)S(1)}, u32[]{:S(2)}, u32[]{:S(2)}) collective-permute-start(bf16[192,1024]{1,0:T(8,128)(2,1)S(1)} %pad_maximum_fusion), channel_id=1, source_target_pairs={{0,128},{64,448},{128,256},{192,64},{256,384},{320,192},{384,0},{4... | collective-permute-start | bytes 1179656 | tf_op jit(solution)/shard_map/ppermute | solution.py:212
  44.8 1.9 %collective-permute-start.2 = (bf16[96,1024]{1,0:T(8,128)(2,1)S(1)}, bf16[96,1024]{1,0:T(8,128)(2,1)S(1)}, u32[]{:S(2)}, u32[]{:S(2)}) collective-permute-start(bf16[96,1024]{1,0:T(8,128)(2,1)S(1)} %convolution_convert_fusion.1.mine), channel_id=1, source_target_pairs={{0,384},{64,192},{128,0},{192,320},{256,128},{320,448},{384,256},{... | collective-permute-start | bytes 589832 | tf_op jit(solution)/shard_map/ppermute | solution.py:212
  46.7 6.3 %collective-permute-done.2.far = bf16[96,1024]{1,0:T(8,128)(2,1)S(1)} collective-permute-done((bf16[96,1024]{1,0:T(8,128)(2,1)S(1)}, bf16[96,1024]{1,0:T(8,128)(2,1)S(1)}, u32[]{:S(2)}, u32[]{:S(2)}) %collective-permute-start.2) | collective-permute-done | bytes 196640 | tf_op jit(solution)/shard_map/ppermute | solution.py:212
  53.0 0.0 collective-permute-done.1.near
  53.0 1.4 %grams.1 = (bf16[1536,128]{1,0:T(8,128)(2,1)S(1)}, bf16[5,128,1024]{2,1,0:T(8,128)(2,1)S(1)}) custom-call(s32[1]{0:T(128)} %bitcast.core, bf16[96,1024]{1,0:T(8,128)(2,1)S(1)} %convolution_convert_fusion.1.mine, bf16[96,1024]{1,0:T(8,128)(2,1)S(1)} %collective-permute-done.partner, bf16[192,1024]{1,0:T(8,128)(2,1)S(1)} %collective-permute-done.1.near, ...), custom_call_target="tpu_custom_call" | custom-call | tf_op jit(solution)/shard_map/grams/pallas_call | solution.py:237
  54.5 20.5 %all_to_all.15 = bf16[64,24,128]{2,1,0:T(8,128)(2,1)S(1)} all-to-all(bf16[64,24,128]{2,1,0:T(8,128)(2,1)S(1)} %bitcast.19), channel_id=1, replica_groups=mesh['col'=8,'row'=64] {'row'}, dimensions={0} | all-to-all | bytes 786432 | tf_op jit(solution)/shard_map/all_to_all | solution.py:249
  75.0 0.1 convert_reduce_fusion
  75.1 0.1 fusion.4
  75.1 0.1 fusion.3
  75.3 22.0 %all_to_all.16 = f32[64,16,128]{2,1,0:T(8,128)S(1)} all-to-all(f32[64,16,128]{2,1,0:T(8,128)S(1)} %broadcast_in_dim.9), channel_id=1, replica_groups=mesh['col'=8,'row'=64] {'row'}, dimensions={0} | all-to-all | bytes 1048576 | tf_op jit(solution)/shard_map/all_to_all | solution.py:252
  97.2 8.8 %rounds.1 = (bf16[96,1024]{1,0:T(8,128)(2,1)S(1)}, bf16[96,1024]{1,0:T(8,128)(2,1)S(1)}) custom-call(s32[1]{0:T(128)} %bitcast.core, f32[1024,128]{1,0:T(8,128)S(1)} %bitcast.18, bf16[5,128,1024]{2,1,0:T(8,128)(2,1)S(1)} %get-tuple-element.10.rows_ref), custom_call_target="tpu_custom_call" | custom-call | tf_op jit(solution)/shard_map/rounds/pallas_call | solution.py:254
  106.1 5.4 %collective-permute-start.3 = (bf16[96,1024]{1,0:T(8,128)(2,1)S(1)}, bf16[96,1024]{1,0:T(8,128)(2,1)S(1)}, u32[]{:S(2)}, u32[]{:S(2)}) collective-permute-start(bf16[96,1024]{1,0:T(8,128)(2,1)S(1)} %get-tuple-element.12), channel_id=1, source_target_pairs={{0,64},{64,0},{128,192},{192,128},{256,320},{320,256},{384,448},{4... | collective-permute-start | bytes 589832 | tf_op jit(solution)/shard_map/ppermute | solution.py:212
  111.5 1.0 collective-permute-done.3
  112.6 0.8 pad_maximum_fusion.1
  (3 shorter events, 0.1 us)
Async XLA Ops:
  0.0 19.0 %copy-start = (s32[192]{0:T(256)S(1)}, s32[192]{0:T(256)}, u32[]{:S(2)}) copy-start(s32[192]{0:T(256)} %param.3) | copy-start | bytes 2308
  1.9 31.8 %all-to-all-start = ((bf16[64,24,128]{2,1,0:T(8,128)(2,1)}), bf16[64,24,128]{2,1,0:T(8,128)(2,1)S(1)}, u32[]{:S(2)}, u32[]{:S(2)}) async-start(bf16[64,24,128]{2,1,0:T(8,128)(2,1)} %copy_bitcast_fusion), calls=%async_computation | async-start | bytes 786432 | tf_op jit(solution)/shard_map/all_to_all | solution.py:222
  34.1 6.3 %collective-permute-start = (bf16[96,1024]{1,0:T(8,128)(2,1)S(1)}, bf16[96,1024]{1,0:T(8,128)(2,1)S(1)}, u32[]{:S(2)}, u32[]{:S(2)}) collective-permute-start(bf16[96,1024]{1,0:T(8,128)(2,1)S(1)} %convolution_convert_fusion), channel_id=1, source_target_pairs={{0,64},{64,0},{128,192},{192,128},{256,320},{320,256},{384,448},{4... | collective-permute-start | bytes 589832 | tf_op jit(solution)/shard_map/ppermute | solution.py:212
  40.4 12.7 %collective-permute-start.1 = (bf16[192,1024]{1,0:T(8,128)(2,1)S(1)}, bf16[192,1024]{1,0:T(8,128)(2,1)S(1)}, u32[]{:S(2)}, u32[]{:S(2)}) collective-permute-start(bf16[192,1024]{1,0:T(8,128)(2,1)S(1)} %pad_maximum_fusion), channel_id=1, source_target_pairs={{0,128},{64,448},{128,256},{192,64},{256,384},{320,192},{384,0},{4... | collective-permute-start | bytes 1179656 | tf_op jit(solution)/shard_map/ppermute | solution.py:212
  44.8 8.3 %collective-permute-start.2 = (bf16[96,1024]{1,0:T(8,128)(2,1)S(1)}, bf16[96,1024]{1,0:T(8,128)(2,1)S(1)}, u32[]{:S(2)}, u32[]{:S(2)}) collective-permute-start(bf16[96,1024]{1,0:T(8,128)(2,1)S(1)} %convolution_convert_fusion.1.mine), channel_id=1, source_target_pairs={{0,384},{64,192},{128,0},{192,320},{256,128},{320,448},{384,256},{... | collective-permute-start | bytes 589832 | tf_op jit(solution)/shard_map/ppermute | solution.py:212
  106.1 6.5 %collective-permute-start.3 = (bf16[96,1024]{1,0:T(8,128)(2,1)S(1)}, bf16[96,1024]{1,0:T(8,128)(2,1)S(1)}, u32[]{:S(2)}, u32[]{:S(2)}) collective-permute-start(bf16[96,1024]{1,0:T(8,128)(2,1)S(1)} %get-tuple-element.12), channel_id=1, source_target_pairs={{0,64},{64,0},{128,192},{192,128},{256,320},{320,256},{384,448},{4... | collective-permute-start | bytes 589832 | tf_op jit(solution)/shard_map/ppermute | solution.py:212

commit v10 on v8

--- a/solution.py
+++ b/solution.py
@@ -221,9 +221,10 @@
     width = frames.shape[1] // row_count
     core = lax.axis_index("col") % 2
     deep = width // LANES
-    tiles = frames.reshape(-1, row_count, deep, LANES).transpose(1, 0, 2, 3)
+    tiles = frames.reshape(-1, row_count, deep, LANES).transpose(1, 2, 0, 3)
     tiles = tiles.reshape(row_count, -1, LANES)
     arrived = lax.all_to_all(tiles, "row", split_axis=0, concat_axis=0, tiled=True)
+    arrived = arrived.reshape(row_count, deep, -1, LANES).transpose(0, 2, 1, 3)
     arrived = arrived.reshape(frame_order.shape[0], width)
     order = jnp.where(core == 0, jnp.roll(frame_order, PAIR), frame_order)
     picks = (order[:, None] == iota((1, order.shape[0]), 1)).astype(jnp.bfloat16)

time: 114 us -> 114 us (level)
  no operation moved by 1% of the time
where the time goes in v10:
time: 114 us
  blocking collectives  42.4 us (37%)
  starting transfers between devices  34.1 us (30%)
  waiting for transfers between devices  22.6 us (20%)
  Pallas kernels  10.3 us (9%)
  local copies, waits for them, and re-layouts  2.71 us (2%)
  other arithmetic  1.17 us (1%)
    all_to_all x1, blocking collectives, on_device(): lax.all_to_all(copies, 'row', split_axis=0, concat_axis=0, tiled=True)  22 us
    all_to_all x1, blocking collectives, on_device(): lax.all_to_all(parts, 'row', split_axis=0, concat_axis=0, tiled=True)  20.5 us
    all_to_all x1, starting transfers between devices, on_device(): lax.all_to_all(tiles, 'row', split_axis=0, concat_axis=0, tiled=True)  17.1 us
    ppermute x4, starting transfers between devices, passed(): lax.ppermute(value, 'col', [(source, where(source) % count) for source in...  17 us
    all_to_all x1, waiting for transfers between devices, on_device(): lax.all_to_all(tiles, 'row', split_axis=0, concat_axis=0, tiled=True)  14.4 us
    pallas_call x1, Pallas kernels, on_device(): pl.pallas_call(rounds_kernel, out_shape=(pair, pair), in_specs=[scalar, v...  8.88 us
    ppermute x4, waiting for transfers between devices, passed(): lax.ppermute(value, 'col', [(source, where(source) % count) for source in...  8.23 us
  transfers between devices with their start and end apart: 5, of which 4 were waited for; matrix products, arithmetic and copies ran while one was open for 0% of the time, Pallas kernels for 0%

profile of v10, /device:TPU:1, one launch (start us, length us, event | category | flops | bytes accessed | tf_op | source)
XLA Modules:
  0.0 113.9 jit_solution(10170283409385637068)
XLA Ops:
  0.0 1.1 copy.21
  1.1 0.0 copy-start
  1.1 0.1 copy.6
  1.2 1.0 copy.7
  2.2 17.1 %all-to-all-start = ((bf16[64,24,128]{2,1,0:T(8,128)(2,1)}), bf16[64,24,128]{2,1,0:T(8,128)(2,1)S(1)}, u32[]{:S(2)}, u32[]{:S(2)}) async-start(bf16[64,24,128]{2,1,0:T(8,128)(2,1)} %copy.7), calls=%async_computation | async-start | bytes 786432 | tf_op jit(solution)/shard_map/all_to_all | solution.py:226
  19.4 0.0 copy-done
  19.4 0.1 fusion.9
  19.4 0.1 add_select_fusion
  19.5 0.1 iota_compare_fusion
  19.6 14.4 %all-to-all-done = bf16[64,24,128]{2,1,0:T(8,128)(2,1)S(1)} async-done(((bf16[64,24,128]{2,1,0:T(8,128)(2,1)}), bf16[64,24,128]{2,1,0:T(8,128)(2,1)S(1)}, u32[]{:S(2)}, u32[]{:S(2)}) %all-to-all-start) | async-done | bytes 393248 | tf_op jit(solution)/shard_map/all_to_all | solution.py:226
  34.0 0.1 copy.8
  34.1 0.3 copy.9
  34.4 0.2 convolution_convert_fusion
  34.6 5.2 %collective-permute-start = (bf16[96,1024]{1,0:T(8,128)(2,1)S(1)}, bf16[96,1024]{1,0:T(8,128)(2,1)S(1)}, u32[]{:S(2)}, u32[]{:S(2)}) collective-permute-start(bf16[96,1024]{1,0:T(8,128)(2,1)S(1)} %convolution_convert_fusion), channel_id=1, source_target_pairs={{0,64},{64,0},{128,192},{192,128},{256,320},{320,256},{384,448},{4... | collective-permute-start | bytes 589832 | tf_op jit(solution)/shard_map/ppermute | solution.py:216
  39.8 0.2 convolution_convert_fusion.1.mine
  40.0 0.8 collective-permute-done.partner
  40.9 4.4 %collective-permute-start.1 = (bf16[192,1024]{1,0:T(8,128)(2,1)S(1)}, bf16[192,1024]{1,0:T(8,128)(2,1)S(1)}, u32[]{:S(2)}, u32[]{:S(2)}) collective-permute-start(bf16[192,1024]{1,0:T(8,128)(2,1)S(1)} %pad_maximum_fusion), channel_id=1, source_target_pairs={{0,128},{64,448},{128,256},{192,64},{256,384},{320,192},{384,0},{4... | collective-permute-start | bytes 1179656 | tf_op jit(solution)/shard_map/ppermute | solution.py:216
  45.3 1.9 %collective-permute-start.2 = (bf16[96,1024]{1,0:T(8,128)(2,1)S(1)}, bf16[96,1024]{1,0:T(8,128)(2,1)S(1)}, u32[]{:S(2)}, u32[]{:S(2)}) collective-permute-start(bf16[96,1024]{1,0:T(8,128)(2,1)S(1)} %convolution_convert_fusion.1.mine), channel_id=1, source_target_pairs={{0,384},{64,192},{128,0},{192,320},{256,128},{320,448},{384,256},{... | collective-permute-start | bytes 589832 | tf_op jit(solution)/shard_map/ppermute | solution.py:216
  47.2 6.3 %collective-permute-done.2.far = bf16[96,1024]{1,0:T(8,128)(2,1)S(1)} collective-permute-done((bf16[96,1024]{1,0:T(8,128)(2,1)S(1)}, bf16[96,1024]{1,0:T(8,128)(2,1)S(1)}, u32[]{:S(2)}, u32[]{:S(2)}) %collective-permute-start.2) | collective-permute-done | bytes 196640 | tf_op jit(solution)/shard_map/ppermute | solution.py:216
  53.6 0.0 collective-permute-done.1.near
  53.6 1.4 %grams.1 = (bf16[1536,128]{1,0:T(8,128)(2,1)S(1)}, bf16[5,128,1024]{2,1,0:T(8,128)(2,1)S(1)}) custom-call(s32[1]{0:T(128)} %bitcast.core, bf16[96,1024]{1,0:T(8,128)(2,1)S(1)} %convolution_convert_fusion.1.mine, bf16[96,1024]{1,0:T(8,128)(2,1)S(1)} %collective-permute-done.partner, bf16[192,1024]{1,0:T(8,128)(2,1)S(1)} %collective-permute-done.1.near, ...), custom_call_target="tpu_custom_call" | custom-call | tf_op jit(solution)/shard_map/grams/pallas_call | solution.py:242
  55.0 20.5 %all_to_all.15 = bf16[64,24,128]{2,1,0:T(8,128)(2,1)S(1)} all-to-all(bf16[64,24,128]{2,1,0:T(8,128)(2,1)S(1)} %bitcast.26), channel_id=1, replica_groups=mesh['col'=8,'row'=64] {'row'}, dimensions={0} | all-to-all | bytes 786432 | tf_op jit(solution)/shard_map/all_to_all | solution.py:254
  75.5 0.1 convert_reduce_fusion
  75.6 0.1 fusion.8
  75.6 0.1 fusion.7
  75.8 22.0 %all_to_all.16 = f32[64,16,128]{2,1,0:T(8,128)S(1)} all-to-all(f32[64,16,128]{2,1,0:T(8,128)S(1)} %broadcast_in_dim.9), channel_id=1, replica_groups=mesh['col'=8,'row'=64] {'row'}, dimensions={0} | all-to-all | bytes 1048576 | tf_op jit(solution)/shard_map/all_to_all | solution.py:257
  97.7 8.9 %rounds.1 = (bf16[96,1024]{1,0:T(8,128)(2,1)S(1)}, bf16[96,1024]{1,0:T(8,128)(2,1)S(1)}) custom-call(s32[1]{0:T(128)} %bitcast.core, f32[1024,128]{1,0:T(8,128)S(1)} %bitcast.25, bf16[5,128,1024]{2,1,0:T(8,128)(2,1)S(1)} %get-tuple-element.10.rows_ref), custom_call_target="tpu_custom_call" | custom-call | tf_op jit(solution)/shard_map/rounds/pallas_call | solution.py:259
  106.6 5.4 %collective-permute-start.3 = (bf16[96,1024]{1,0:T(8,128)(2,1)S(1)}, bf16[96,1024]{1,0:T(8,128)(2,1)S(1)}, u32[]{:S(2)}, u32[]{:S(2)}) collective-permute-start(bf16[96,1024]{1,0:T(8,128)(2,1)S(1)} %get-tuple-element.12), channel_id=1, source_target_pairs={{0,64},{64,0},{128,192},{192,128},{256,320},{320,256},{384,448},{4... | collective-permute-start | bytes 589832 | tf_op jit(solution)/shard_map/ppermute | solution.py:216
  112.1 1.0 collective-permute-done.3
  113.1 0.8 pad_maximum_fusion.1
  (3 shorter events, 0.1 us)
Async XLA Ops:
  1.1 18.3 %copy-start = (s32[192]{0:T(256)S(1)}, s32[192]{0:T(256)}, u32[]{:S(2)}) copy-start(s32[192]{0:T(256)} %param.3) | copy-start | bytes 2308
  2.2 31.8 %all-to-all-start = ((bf16[64,24,128]{2,1,0:T(8,128)(2,1)}), bf16[64,24,128]{2,1,0:T(8,128)(2,1)S(1)}, u32[]{:S(2)}, u32[]{:S(2)}) async-start(bf16[64,24,128]{2,1,0:T(8,128)(2,1)} %copy.7), calls=%async_computation | async-start | bytes 786432 | tf_op jit(solution)/shard_map/all_to_all | solution.py:226
  34.6 6.3 %collective-permute-start = (bf16[96,1024]{1,0:T(8,128)(2,1)S(1)}, bf16[96,1024]{1,0:T(8,128)(2,1)S(1)}, u32[]{:S(2)}, u32[]{:S(2)}) collective-permute-start(bf16[96,1024]{1,0:T(8,128)(2,1)S(1)} %convolution_convert_fusion), channel_id=1, source_target_pairs={{0,64},{64,0},{128,192},{192,128},{256,320},{320,256},{384,448},{4... | collective-permute-start | bytes 589832 | tf_op jit(solution)/shard_map/ppermute | solution.py:216
  40.9 12.7 %collective-permute-start.1 = (bf16[192,1024]{1,0:T(8,128)(2,1)S(1)}, bf16[192,1024]{1,0:T(8,128)(2,1)S(1)}, u32[]{:S(2)}, u32[]{:S(2)}) collective-permute-start(bf16[192,1024]{1,0:T(8,128)(2,1)S(1)} %pad_maximum_fusion), channel_id=1, source_target_pairs={{0,128},{64,448},{128,256},{192,64},{256,384},{320,192},{384,0},{4... | collective-permute-start | bytes 1179656 | tf_op jit(solution)/shard_map/ppermute | solution.py:216
  45.3 8.3 %collective-permute-start.2 = (bf16[96,1024]{1,0:T(8,128)(2,1)S(1)}, bf16[96,1024]{1,0:T(8,128)(2,1)S(1)}, u32[]{:S(2)}, u32[]{:S(2)}) collective-permute-start(bf16[96,1024]{1,0:T(8,128)(2,1)S(1)} %convolution_convert_fusion.1.mine), channel_id=1, source_target_pairs={{0,384},{64,192},{128,0},{192,320},{256,128},{320,448},{384,256},{... | collective-permute-start | bytes 589832 | tf_op jit(solution)/shard_map/ppermute | solution.py:216
  106.6 6.5 %collective-permute-start.3 = (bf16[96,1024]{1,0:T(8,128)(2,1)S(1)}, bf16[96,1024]{1,0:T(8,128)(2,1)S(1)}, u32[]{:S(2)}, u32[]{:S(2)}) collective-permute-start(bf16[96,1024]{1,0:T(8,128)(2,1)S(1)} %get-tuple-element.12), channel_id=1, source_target_pairs={{0,64},{64,0},{128,192},{192,128},{256,320},{320,256},{384,448},{4... | collective-permute-start | bytes 589832 | tf_op jit(solution)/shard_map/ppermute | solution.py:216
